TPU v7x, 128 devices: a whole 4x4x4 slice. The times are simulated.
128 devices in a mesh: seq: 32 (over z, y, core), enc: 4 (over x).
Axes of the slice: x: 4, y: 4, z: 4, core: 2. Of those that a mesh axis runs over, the one named last changes fastest.
Arguments:
- enc_tiles: bfloat16 [32, 4, 1601, 1280], P('seq', 'enc'), may hold values from -6 to 6
- kv_weight: bfloat16 [1280, 1024], replicated, may hold values from -0.15625 to 0.15625
- q_cross: bfloat16 [4096, 4096], P('seq', 'enc'), may hold values from -210 to 210
- q_self: bfloat16 [4096, 4096], P('seq', 'enc'), may hold values from -210 to 210
- self_cache: bfloat16 [4, 256, 4096], P('enc', 'seq'), may hold values from -6 to 6
- image_range: int32 [64, 2], P('seq'), may hold values from 0 to 32, as said below
- image_tiles: int32 [32], replicated, may hold values from 1 to 4
Outputs:
- cross_context: bfloat16 [4096, 4096], P('seq', 'enc')
- self_context: bfloat16 [4096, 4096], P('seq', 'enc')
- cache_seq: bfloat16 [4, 256, 4096], P('enc', None, 'seq')
Inputs may be any that keep to these rules, and one draw needn't show every extreme that they name: With s = c // 2, span c sees one or two images: s - 1 <= image_range[c, 0] < image_range[c, 1] <= s + 1.
All inputs are finite; a program needn't handle non-finite values.
Results may differ from a plain program's by a relative error of at most 0.012.
The roundings to bfloat16 on the way count: a program that leaves them out, or rounds other values in their place, can miss the bound.
Values may be sent and summed in bfloat16 or wider, within the bound.
No kernel may reach another device: no remote copies, remote signals or barrier semaphores. Data moves between devices by JAX's collectives and lax.ppermute only.
A program may use at most 128 MiB of HBM per device.

v0:
```python
import math

import jax
import jax.numpy as jnp
from jax import lax
from jax.sharding import PartitionSpec as P

HD = 128


NEG_FILL = -1e30


def from_behind(x, axis, by):
    size = lax.axis_size(axis)
    pairs = [(i, i + by) for i in range(size) if 0 <= i + by < size]
    return lax.ppermute(x, axis, pairs)


def lookup_entry(table, position):
    return jnp.sum(jnp.where(jnp.arange(table.shape[0], dtype=jnp.int32) == position, table, 0))


def partial_head(query_rows, key_rows, value_rows, allowed):
    scores = lax.dot_general(
        query_rows, key_rows, (((1,), (1,)), ((), ())), preferred_element_type=jnp.float32
    ) * (1.0 / math.sqrt(HD))
    guarded = jnp.where(allowed, scores, NEG_FILL)
    row_max = jnp.max(guarded, axis=-1)
    exponent = jnp.where(allowed, jnp.exp(guarded - row_max[:, None]), 0.0)
    row_sum = jnp.sum(exponent, axis=-1)
    mixed = jnp.dot(exponent.astype(jnp.bfloat16), value_rows, preferred_element_type=jnp.float32)
    return (row_max, row_sum, mixed)


def on_device(enc_tiles, kv_weight, q_cross, q_self, self_cache, image_range, image_tiles):
    seq_index = lax.axis_index("seq")
    row_count = q_cross.shape[0]
    group_size = q_cross.shape[1] // HD
    tile_rows = enc_tiles.shape[2]
    score_scale = 1.0 / math.sqrt(HD)
    kv_tile = jnp.dot(enc_tiles[0, 0], kv_weight, preferred_element_type=jnp.float32).astype(
        jnp.bfloat16
    )
    own_image = lax.all_to_all(kv_tile, "enc", split_axis=1, concat_axis=0, tiled=True)
    key_width = own_image.shape[0]
    positions = jnp.arange(key_width, dtype=jnp.int32)
    prev_tokens = lookup_entry(image_tiles, seq_index - 1) * tile_rows
    own_tokens = lookup_entry(image_tiles, seq_index) * tile_rows
    lower_rows = jnp.repeat(image_range[:, 0], row_count // image_range.shape[0])
    upper_rows = jnp.repeat(image_range[:, 1], row_count // image_range.shape[0])
    prev_live = (lower_rows <= seq_index - 1) & (upper_rows > seq_index - 1)
    own_live = (lower_rows <= seq_index) & (upper_rows > seq_index)
    own_allowed = own_live[:, None] & (positions[None, :] < own_tokens)
    cross_queries = jnp.transpose(q_cross.reshape(row_count, group_size, HD), (1, 0, 2))
    prev_kv = from_behind(own_image, "seq", 1)
    image_pair = jnp.concatenate([prev_kv, own_image], 0)
    allowed_cross = jnp.concatenate(
        [prev_live[:, None] & (positions[None, :] < prev_tokens), own_allowed], 1
    )
    pair_keys = image_pair[:, :HD]
    pair_values = image_pair[:, HD:]

    def cross_head(query_rows):
        row_max, row_sum, mixed = partial_head(query_rows, pair_keys, pair_values, allowed_cross)
        return mixed / row_sum[:, None]

    cross_heads = lax.map(cross_head, cross_queries)
    cross_context = (
        jnp.transpose(cross_heads, (1, 0, 2))
        .reshape(row_count, group_size * HD)
        .astype(jnp.bfloat16)
    )
    cache_seq = lax.all_to_all(self_cache, "seq", split_axis=2, concat_axis=1, tiled=True)
    self_queries = jnp.transpose(q_self.reshape(row_count, group_size, HD), (1, 0, 2))
    row_start = seq_index * row_count
    row_pos = row_start + jnp.arange(row_count, dtype=jnp.int32)

    def update(carry_state, key_rows, value_rows, key_start):
        running_max, running_sum, weighted = carry_state
        scores = (
            jnp.einsum("grd,dn->grn", self_queries, key_rows, preferred_element_type=jnp.float32)
            * score_scale
        )
        key_pos = key_start + jnp.arange(key_rows.shape[1], dtype=jnp.int32)
        allowed = key_pos[None, :] <= row_pos[:, None]
        guarded = jnp.where(allowed[None], scores, NEG_FILL)
        new_max = jnp.maximum(running_max, jnp.max(guarded, axis=-1))
        exponent = jnp.where(allowed[None], jnp.exp(guarded - new_max[..., None]), 0.0)
        decay_factor = jnp.exp(running_max - new_max)
        running_sum = running_sum * decay_factor + jnp.sum(exponent, axis=-1)
        weighted = weighted * decay_factor[..., None] + jnp.einsum(
            "grn,dn->grd",
            exponent.astype(jnp.bfloat16),
            value_rows,
            preferred_element_type=jnp.float32,
        )
        return (new_max, running_sum, weighted)

    def visit(carry_state, key_rows, value_rows, key_start):
        return update(carry_state, key_rows, value_rows, key_start)

    init_state = (
        jnp.full((group_size, row_count), NEG_FILL, jnp.float32),
        jnp.zeros((group_size, row_count), jnp.float32),
        jnp.zeros((group_size, row_count, HD), jnp.float32),
    )
    piece = lax.all_gather(cache_seq, "seq", axis=2, tiled=True)
    key_rows = piece[0, :HD]
    value_rows = piece[0, HD:]
    count_keys = key_rows.shape[1]
    block_size = min(512, count_keys)
    block_count = count_keys // block_size

    def one_block(block_index, inner_state):
        offset = block_index * block_size
        return visit(
            inner_state,
            lax.dynamic_slice_in_dim(key_rows, offset, block_size, 1),
            lax.dynamic_slice_in_dim(value_rows, offset, block_size, 1),
            offset,
        )

    final_state = lax.fori_loop(0, block_count, one_block, init_state)
    self_heads = final_state[2] / final_state[1][..., None]
    self_context = (
        jnp.transpose(self_heads, (1, 0, 2))
        .reshape(row_count, group_size * HD)
        .astype(jnp.bfloat16)
    )
    return (cross_context, self_context, cache_seq)


def solution(mesh):
    return jax.shard_map(
        on_device,
        mesh=mesh,
        in_specs=(
            P("seq", "enc", None, None),
            P(),
            P("seq", "enc"),
            P("seq", "enc"),
            P("enc", "seq", None),
            P("seq", None),
            P(),
        ),
        out_specs=(P("seq", "enc"), P("seq", "enc"), P("enc", None, "seq")),
        check_vma=False,
    )
```

profile of v0, /device:TPU:65, one launch (start us, length us, event | category | flops | bytes accessed | tf_op | source)
XLA Modules:
  0.0 296.1 jit_solution(2618760349952761615)
XLA Ops:
  7.2 5.0 %copy.51 = bf16[1,8,4096]{1,0,2:T(2,128)(2,1)} copy(bf16[1,8,4096]{2,1,0:T(8,128)(2,1)} %param.15) | data formatting | bytes 131072 | tf_op args[4]
  12.8 24.4 %reduce.4 = bf16[4096,8]{1,0:T(8,128)(2,1)} reduce(bf16[4096,1,8]{2,1,0:T(2,128)(2,1)} %bitcast.98, bf16[]{:T(256)} %broadcast.131), dimensions={1}, to_apply=%bitcast.62.reduce_sub_computation | reduce | bytes 131074
  39.7 13.3 %all_to_all.37 = bf16[32,2,512]{2,1,0:T(2,128)(2,1)S(1)} all-to-all(bf16[32,2,512]{2,1,0:T(2,128)(2,1)S(1)} %reshape.116), channel_id=1, replica_groups=mesh['seq'=32,'enc'=4] {'seq'}, dimensions={0} | all-to-all | bytes 131072 | tf_op jit(solution)/shard_map/all_to_all | solution.py:74
  53.0 4.5 %reshape.117 = bf16[4096,1,8]{2,1,0:T(2,128)(2,1)} reshape(bf16[32,2,512]{2,1,0:T(2,128)(2,1)S(1)} %all_to_all.37) | data formatting | bytes 131072
  57.5 4.4 %copy.52 = bf16[1,8,4096]{2,1,0:T(8,128)(2,1)S(1)} copy(bf16[1,8,4096]{1,0,2:T(2,128)(2,1)} %bitcast.99) | data formatting | bytes 131072 | tf_op jit(solution)/shard_map/all_to_all | solution.py:74
  62.6 8.1 %fusion.43 = bf16[1601,1024]{1,0:T(8,128)(2,1)} fusion(bf16[1280,1024]{1,0:T(8,128)(2,1)S(1)} %copy-done, bf16[1,1,1601,1280]{3,2,1,0:T(8,128)(2,1)} %param.11), kind=kOutput, calls=%fused_computation.49 | convolution fusion | flops 4198564864 | bytes 9998848 | tf_op jit(solution)/shard_map/dot_general | solution.py:42
  70.7 7.1 %all_to_all.27 = bf16[1601,4,256]{2,1,0:T(4,128)(2,1)} reshape(bf16[1601,1024]{1,0:T(8,128)(2,1)} %fusion.43) | data formatting | bytes 6557696 | tf_op jit(solution)/shard_map/all_to_all | solution.py:45
  77.8 4.1 %copy.48 = bf16[1601,4,256]{2,0,1:T(8,128)(2,1)} copy(bf16[1601,4,256]{2,1,0:T(4,128)(2,1)} %all_to_all.27) | data formatting | bytes 6557696 | tf_op jit(solution)/shard_map/all_to_all | solution.py:45
  82.0 5.0 %all-to-all-start = ((bf16[1601,4,256]{2,0,1:T(8,128)(2,1)}), bf16[1601,4,256]{2,0,1:T(8,128)(2,1)}, u32[]{:S(2)}, u32[]{:S(2)}) async-start(bf16[1601,4,256]{2,0,1:T(8,128)(2,1)} %copy.48), calls=%async_computation | async-start | bytes 6586368 | tf_op jit(solution)/shard_map/all_to_all | solution.py:45
  91.0 4.2 %broadcast_and_fusion = (pred[128,6404]{0,1:T(8,128)(4,1)S(1)}, pred[128,6404]{0,1:T(8,128)(4,1)S(1)}) fusion(pred[128]{0:T(512)(128)(4,1)S(1)} %and.63, pred[6404]{0:T(1024)(128)(4,1)S(1)} %iota_compare_fusion, pred[6404]{0:T(1024)(128)(4,1)S(1)} %iota_compare_fusion.1, pred[128]{0:T(512)(128)(4,1)S(1)} %and.57), kind=kLoop, calls=%fused_computation.52 | loop fusion | flops 1639424 | bytes 1652488 | tf_op jit(solution)/shard_map/and | solution.py:54
  95.1 13.6 %pad_add_fusion = pred[128,12808]{0,1:T(8,128)(4,1)} fusion(pred[128,6404]{0,1:T(8,128)(4,1)S(1)} %get-tuple-element.314, pred[128,6404]{0,1:T(8,128)(4,1)S(1)} %get-tuple-element.315), kind=kLoop, calls=%fused_computation.46 | loop fusion | flops 1639424 | bytes 3278848 | tf_op jit(solution)/shard_map/concatenate | solution.py:58
  108.8 16.9 %all-to-all-done = bf16[1601,4,256]{2,0,1:T(8,128)(2,1)} async-done(((bf16[1601,4,256]{2,0,1:T(8,128)(2,1)}), bf16[1601,4,256]{2,0,1:T(8,128)(2,1)}, u32[]{:S(2)}, u32[]{:S(2)}) %all-to-all-start) | async-done | bytes 3278880 | tf_op jit(solution)/shard_map/all_to_all | solution.py:45
  125.7 4.5 %all_to_all.30 = bf16[6404,256]{1,0:T(8,128)(2,1)} reshape(bf16[4,1601,256]{2,1,0:T(8,128)(2,1)} %bitcast.5) | data formatting | bytes 6557696 | tf_op jit(solution)/shard_map/all_to_all | solution.py:45
  130.2 3.5 %collective-permute-start = (bf16[6404,256]{1,0:T(8,128)(2,1)}, bf16[6404,256]{1,0:T(8,128)(2,1)}, u32[]{:S(2)}, u32[]{:S(2)}) collective-permute-start(bf16[6404,256]{1,0:T(8,128)(2,1)} %all_to_all.30), channel_id=1, source_target_pairs={{0,4},{4,8},{8,12},{12,16},{16,20},{20,24},{24,28},{28,32},{32,36}... | collective-permute-start | bytes 9836552 | tf_op jit(solution)/shard_map/ppermute | solution.py:17
  136.9 66.3 %while.29 = (s32[]{:T(128)}, f32[8,128]{1,0:T(8,128)S(1)}, f32[8,128]{1,0:T(8,128)S(1)}, f32[8,128,128]{2,1,0:T(8,128)}, bf16[128,4096]{1,0:T(8,128)(2,1)}, /*in...) while((s32[]{:T(128)}, f32[8,128]{1,0:T(8,128)S(1)}, ...), condition=%wide.region_9.10_spmd.clone, body=%wide.region_6.9_spmd.clone.sunk | while | flops 275715712 | bytes 8197311 | solution.py:124
  150.1 3.3 %convolution_add_fusion.2 = f32[8,128,128]{2,1,0:T(8,128)} fusion(f32[512,8,128]{2,0,1:T(8,128)} %get-tuple-element.411, f32[8,128]{1,0:T(8,128)S(1)} %select_maximum_fusion.2, pred[128,512]{0,1:T(8,128)(4,1)S(1)} %broadcast_compare_fusion.2, f32[8,128,128]{2,1,0:T(8,128)} %get-tuple-element.450, f32[8,128]{1,0:T(8,128)S(1)} %get-tuple-element.413, ...), kind=kOutput, calls=%fused_computation.21.clone.1 | convolution fusion | flops 137232384 | bytes 3350533 | tf_op jit(solution)/shard_map/while/body/eval_jaxpr/grn,dn->grd/dot_general | solution.py:92
  158.4 3.3 %convolution_add_fusion.2 = f32[8,128,128]{2,1,0:T(8,128)} fusion(f32[512,8,128]{2,0,1:T(8,128)} %get-tuple-element.411, f32[8,128]{1,0:T(8,128)S(1)} %select_maximum_fusion.2, pred[128,512]{0,1:T(8,128)(4,1)S(1)} %broadcast_compare_fusion.2, f32[8,128,128]{2,1,0:T(8,128)} %get-tuple-element.450, f32[8,128]{1,0:T(8,128)S(1)} %get-tuple-element.413, ...), kind=kOutput, calls=%fused_computation.21.clone.1 | convolution fusion | flops 137232384 | bytes 3350533 | tf_op jit(solution)/shard_map/while/body/eval_jaxpr/grn,dn->grd/dot_general | solution.py:92
  166.7 3.3 %convolution_add_fusion.2 = f32[8,128,128]{2,1,0:T(8,128)} fusion(f32[512,8,128]{2,0,1:T(8,128)} %get-tuple-element.411, f32[8,128]{1,0:T(8,128)S(1)} %select_maximum_fusion.2, pred[128,512]{0,1:T(8,128)(4,1)S(1)} %broadcast_compare_fusion.2, f32[8,128,128]{2,1,0:T(8,128)} %get-tuple-element.450, f32[8,128]{1,0:T(8,128)S(1)} %get-tuple-element.413, ...), kind=kOutput, calls=%fused_computation.21.clone.1 | convolution fusion | flops 137232384 | bytes 3350533 | tf_op jit(solution)/shard_map/while/body/eval_jaxpr/grn,dn->grd/dot_general | solution.py:92
  175.0 3.3 %convolution_add_fusion.2 = f32[8,128,128]{2,1,0:T(8,128)} fusion(f32[512,8,128]{2,0,1:T(8,128)} %get-tuple-element.411, f32[8,128]{1,0:T(8,128)S(1)} %select_maximum_fusion.2, pred[128,512]{0,1:T(8,128)(4,1)S(1)} %broadcast_compare_fusion.2, f32[8,128,128]{2,1,0:T(8,128)} %get-tuple-element.450, f32[8,128]{1,0:T(8,128)S(1)} %get-tuple-element.413, ...), kind=kOutput, calls=%fused_computation.21.clone.1 | convolution fusion | flops 137232384 | bytes 3350533 | tf_op jit(solution)/shard_map/while/body/eval_jaxpr/grn,dn->grd/dot_general | solution.py:92
  183.3 3.3 %convolution_add_fusion.2 = f32[8,128,128]{2,1,0:T(8,128)} fusion(f32[512,8,128]{2,0,1:T(8,128)} %get-tuple-element.411, f32[8,128]{1,0:T(8,128)S(1)} %select_maximum_fusion.2, pred[128,512]{0,1:T(8,128)(4,1)S(1)} %broadcast_compare_fusion.2, f32[8,128,128]{2,1,0:T(8,128)} %get-tuple-element.450, f32[8,128]{1,0:T(8,128)S(1)} %get-tuple-element.413, ...), kind=kOutput, calls=%fused_computation.21.clone.1 | convolution fusion | flops 137232384 | bytes 3350533 | tf_op jit(solution)/shard_map/while/body/eval_jaxpr/grn,dn->grd/dot_general | solution.py:92
  191.6 3.3 %convolution_add_fusion.2 = f32[8,128,128]{2,1,0:T(8,128)} fusion(f32[512,8,128]{2,0,1:T(8,128)} %get-tuple-element.411, f32[8,128]{1,0:T(8,128)S(1)} %select_maximum_fusion.2, pred[128,512]{0,1:T(8,128)(4,1)S(1)} %broadcast_compare_fusion.2, f32[8,128,128]{2,1,0:T(8,128)} %get-tuple-element.450, f32[8,128]{1,0:T(8,128)S(1)} %get-tuple-element.413, ...), kind=kOutput, calls=%fused_computation.21.clone.1 | convolution fusion | flops 137232384 | bytes 3350533 | tf_op jit(solution)/shard_map/while/body/eval_jaxpr/grn,dn->grd/dot_general | solution.py:92
  199.8 3.3 %convolution_add_fusion.2 = f32[8,128,128]{2,1,0:T(8,128)} fusion(f32[512,8,128]{2,0,1:T(8,128)} %get-tuple-element.411, f32[8,128]{1,0:T(8,128)S(1)} %select_maximum_fusion.2, pred[128,512]{0,1:T(8,128)(4,1)S(1)} %broadcast_compare_fusion.2, f32[8,128,128]{2,1,0:T(8,128)} %get-tuple-element.450, f32[8,128]{1,0:T(8,128)S(1)} %get-tuple-element.413, ...), kind=kOutput, calls=%fused_computation.21.clone.1 | convolution fusion | flops 137232384 | bytes 3350533 | tf_op jit(solution)/shard_map/while/body/eval_jaxpr/grn,dn->grd/dot_general | solution.py:92
  205.1 9.6 %pad_maximum_fusion = (bf16[12808,128]{1,0:T(8,128)(2,1)}, bf16[12808,128]{1,0:T(8,128)(2,1)}) fusion(bf16[6404,256]{1,0:T(8,128)(2,1)} %all_to_all.30, bf16[6404,256]{1,0:T(8,128)(2,1)} %collective-permute-done), kind=kLoop, calls=%fused_computation.51 | loop fusion | flops 13115392 | bytes 13115392 | tf_op jit(solution)/shard_map/concatenate | solution.py:57
  214.7 73.8 %while.28 = (s32[]{:T(128)}, bf16[8,128,128]{2,1,0:T(8,128)(2,1)S(1)}, bf16[8,128,128]{1,2,0:T(8,128)(2,1)S(1)}, bf16[12808,128]{1,0:T(8,128)(2,1)}, pred[128,12...) while((s32[]{:T(128)}, bf16[8,128,128]{2,1,0:T(8,128)(2,1)S(1)}, ...), condition=%wide.region_5.6_spmd, body=%wide.region_2.5_spmd.sunk | while | flops 854156032 | bytes 50923148 | solution.py:68
  214.7 4.9 %fusion.72 = (f32[128]{0:T(128)S(1)}, f32[128,12808]{0,1:T(8,128)S(1)}) fusion(pred[128,12808]{0,1:T(8,128)(4,1)} %get-tuple-element.432, bf16[12808,128]{1,0:T(8,128)(2,1)} %get-tuple-element.431, bf16[8,128,128]{1,2,0:T(8,128)(2,1)S(1)} %get-tuple-element.430, s32[]{:T(128)} %get-tuple-element.421), kind=kOutput, calls=%fused_computation.71.clone.1 | convolution fusion | flops 424610688 | bytes 11509252 | tf_op jit(solution)/shard_map/while/body/eval_jaxpr/dot_general | solution.py:25
  224.0 4.9 %fusion.72 = (f32[128]{0:T(128)S(1)}, f32[128,12808]{0,1:T(8,128)S(1)}) fusion(pred[128,12808]{0,1:T(8,128)(4,1)} %get-tuple-element.432, bf16[12808,128]{1,0:T(8,128)(2,1)} %get-tuple-element.431, bf16[8,128,128]{1,2,0:T(8,128)(2,1)S(1)} %get-tuple-element.430, s32[]{:T(128)} %get-tuple-element.421), kind=kOutput, calls=%fused_computation.71.clone.1 | convolution fusion | flops 424610688 | bytes 11509252 | tf_op jit(solution)/shard_map/while/body/eval_jaxpr/dot_general | solution.py:25
  233.2 4.9 %fusion.72 = (f32[128]{0:T(128)S(1)}, f32[128,12808]{0,1:T(8,128)S(1)}) fusion(pred[128,12808]{0,1:T(8,128)(4,1)} %get-tuple-element.432, bf16[12808,128]{1,0:T(8,128)(2,1)} %get-tuple-element.431, bf16[8,128,128]{1,2,0:T(8,128)(2,1)S(1)} %get-tuple-element.430, s32[]{:T(128)} %get-tuple-element.421), kind=kOutput, calls=%fused_computation.71.clone.1 | convolution fusion | flops 424610688 | bytes 11509252 | tf_op jit(solution)/shard_map/while/body/eval_jaxpr/dot_general | solution.py:25
  242.4 4.9 %fusion.72 = (f32[128]{0:T(128)S(1)}, f32[128,12808]{0,1:T(8,128)S(1)}) fusion(pred[128,12808]{0,1:T(8,128)(4,1)} %get-tuple-element.432, bf16[12808,128]{1,0:T(8,128)(2,1)} %get-tuple-element.431, bf16[8,128,128]{1,2,0:T(8,128)(2,1)S(1)} %get-tuple-element.430, s32[]{:T(128)} %get-tuple-element.421), kind=kOutput, calls=%fused_computation.71.clone.1 | convolution fusion | flops 424610688 | bytes 11509252 | tf_op jit(solution)/shard_map/while/body/eval_jaxpr/dot_general | solution.py:25
  251.6 4.9 %fusion.72 = (f32[128]{0:T(128)S(1)}, f32[128,12808]{0,1:T(8,128)S(1)}) fusion(pred[128,12808]{0,1:T(8,128)(4,1)} %get-tuple-element.432, bf16[12808,128]{1,0:T(8,128)(2,1)} %get-tuple-element.431, bf16[8,128,128]{1,2,0:T(8,128)(2,1)S(1)} %get-tuple-element.430, s32[]{:T(128)} %get-tuple-element.421), kind=kOutput, calls=%fused_computation.71.clone.1 | convolution fusion | flops 424610688 | bytes 11509252 | tf_op jit(solution)/shard_map/while/body/eval_jaxpr/dot_general | solution.py:25
  260.9 4.9 %fusion.72 = (f32[128]{0:T(128)S(1)}, f32[128,12808]{0,1:T(8,128)S(1)}) fusion(pred[128,12808]{0,1:T(8,128)(4,1)} %get-tuple-element.432, bf16[12808,128]{1,0:T(8,128)(2,1)} %get-tuple-element.431, bf16[8,128,128]{1,2,0:T(8,128)(2,1)S(1)} %get-tuple-element.430, s32[]{:T(128)} %get-tuple-element.421), kind=kOutput, calls=%fused_computation.71.clone.1 | convolution fusion | flops 424610688 | bytes 11509252 | tf_op jit(solution)/shard_map/while/body/eval_jaxpr/dot_general | solution.py:25
  270.1 4.9 %fusion.72 = (f32[128]{0:T(128)S(1)}, f32[128,12808]{0,1:T(8,128)S(1)}) fusion(pred[128,12808]{0,1:T(8,128)(4,1)} %get-tuple-element.432, bf16[12808,128]{1,0:T(8,128)(2,1)} %get-tuple-element.431, bf16[8,128,128]{1,2,0:T(8,128)(2,1)S(1)} %get-tuple-element.430, s32[]{:T(128)} %get-tuple-element.421), kind=kOutput, calls=%fused_computation.71.clone.1 | convolution fusion | flops 424610688 | bytes 11509252 | tf_op jit(solution)/shard_map/while/body/eval_jaxpr/dot_general | solution.py:25
  279.3 4.9 %fusion.72 = (f32[128]{0:T(128)S(1)}, f32[128,12808]{0,1:T(8,128)S(1)}) fusion(pred[128,12808]{0,1:T(8,128)(4,1)} %get-tuple-element.432, bf16[12808,128]{1,0:T(8,128)(2,1)} %get-tuple-element.431, bf16[8,128,128]{1,2,0:T(8,128)(2,1)S(1)} %get-tuple-element.430, s32[]{:T(128)} %get-tuple-element.421), kind=kOutput, calls=%fused_computation.71.clone.1 | convolution fusion | flops 424610688 | bytes 11509252 | tf_op jit(solution)/shard_map/while/body/eval_jaxpr/dot_general | solution.py:25
  (149 shorter events, 89.6 us)
Async XLA Ops:
  7.2 55.4 %copy-start = (bf16[1280,1024]{1,0:T(8,128)(2,1)S(1)}, bf16[1280,1024]{1,0:T(8,128)(2,1)}, u32[]{:S(2)}) copy-start(bf16[1280,1024]{1,0:T(8,128)(2,1)} %param.12) | copy-start | bytes 7864324
  7.2 126.6 %all-gather.2.cloned.1.call-start = ((), (), s32[]{:S(2)}) async-start(), calls=%async_computation.2 | async-start | bytes 2162688 | tf_op jit(solution)/shard_map/all_gather | solution.py:108
  82.0 5.0 %copy-start.6 = (s32[32]{0:T(128)S(1)}, s32[32]{0:T(128)}, u32[]{:S(2)}) copy-start(s32[32]{0:T(128)} %param.17) | copy-start | bytes 388
  82.0 7.0 %copy-start.5 = (s32[2,2]{1,0:T(2,128)S(1)}, s32[2,2]{1,0:T(2,128)}, u32[]{:S(2)}) copy-start(s32[2,2]{1,0:T(2,128)} %param.16) | copy-start | bytes 52
  82.0 7.5 %copy-start.3 = (bf16[128,1024]{1,0:T(8,128)(2,1)S(1)}, bf16[128,1024]{1,0:T(8,128)(2,1)}, u32[]{:S(2)}) copy-start(bf16[128,1024]{1,0:T(8,128)(2,1)} %param.13) | copy-start | bytes 786436
  82.0 43.7 %all-to-all-start = ((bf16[1601,4,256]{2,0,1:T(8,128)(2,1)}), bf16[1601,4,256]{2,0,1:T(8,128)(2,1)}, u32[]{:S(2)}, u32[]{:S(2)}) async-start(bf16[1601,4,256]{2,0,1:T(8,128)(2,1)} %copy.48), calls=%async_computation | async-start | bytes 6586368 | tf_op jit(solution)/shard_map/all_to_all | solution.py:45
  130.2 74.9 %collective-permute-start = (bf16[6404,256]{1,0:T(8,128)(2,1)}, bf16[6404,256]{1,0:T(8,128)(2,1)}, u32[]{:S(2)}, u32[]{:S(2)}) collective-permute-start(bf16[6404,256]{1,0:T(8,128)(2,1)} %all_to_all.30), channel_id=1, source_target_pairs={{0,4},{4,8},{8,12},{12,16},{16,20},{20,24},{24,28},{28,32},{32,36}... | collective-permute-start | bytes 9836552 | tf_op jit(solution)/shard_map/ppermute | solution.py:17
  205.1 9.6 %copy-start.4 = (bf16[8,128,128]{2,1,0:T(8,128)(2,1)S(1)}, bf16[8,128,128]{2,1,0:T(8,128)(2,1)}, u32[]{:S(2)}) copy-start(bf16[8,128,128]{2,1,0:T(8,128)(2,1)} %custom-call.3) | copy-start | bytes 786436
  214.7 4.9 %copy-start.1 = (pred[128,12808]{0,1:T(8,128)(4,1)S(1)}, pred[128,12808]{0,1:T(8,128)(4,1)}, u32[]{:S(2)}) copy-start(pred[128,12808]{0,1:T(8,128)(4,1)} %get-tuple-element.432) | copy-start | bytes 4918276 | tf_op jit(solution)/shard_map/while
  219.6 1.9 copy-start.2
  223.9 4.9 %copy-start.1 = (pred[128,12808]{0,1:T(8,128)(4,1)S(1)}, pred[128,12808]{0,1:T(8,128)(4,1)}, u32[]{:S(2)}) copy-start(pred[128,12808]{0,1:T(8,128)(4,1)} %get-tuple-element.432) | copy-start | bytes 4918276 | tf_op jit(solution)/shard_map/while
  228.9 1.9 copy-start.2
  233.2 4.9 %copy-start.1 = (pred[128,12808]{0,1:T(8,128)(4,1)S(1)}, pred[128,12808]{0,1:T(8,128)(4,1)}, u32[]{:S(2)}) copy-start(pred[128,12808]{0,1:T(8,128)(4,1)} %get-tuple-element.432) | copy-start | bytes 4918276 | tf_op jit(solution)/shard_map/while
  238.1 1.9 copy-start.2
  242.4 4.9 %copy-start.1 = (pred[128,12808]{0,1:T(8,128)(4,1)S(1)}, pred[128,12808]{0,1:T(8,128)(4,1)}, u32[]{:S(2)}) copy-start(pred[128,12808]{0,1:T(8,128)(4,1)} %get-tuple-element.432) | copy-start | bytes 4918276 | tf_op jit(solution)/shard_map/while
  247.3 1.9 copy-start.2
  251.6 4.9 %copy-start.1 = (pred[128,12808]{0,1:T(8,128)(4,1)S(1)}, pred[128,12808]{0,1:T(8,128)(4,1)}, u32[]{:S(2)}) copy-start(pred[128,12808]{0,1:T(8,128)(4,1)} %get-tuple-element.432) | copy-start | bytes 4918276 | tf_op jit(solution)/shard_map/while
  256.6 1.9 copy-start.2
  260.9 4.9 %copy-start.1 = (pred[128,12808]{0,1:T(8,128)(4,1)S(1)}, pred[128,12808]{0,1:T(8,128)(4,1)}, u32[]{:S(2)}) copy-start(pred[128,12808]{0,1:T(8,128)(4,1)} %get-tuple-element.432) | copy-start | bytes 4918276 | tf_op jit(solution)/shard_map/while
  265.8 1.9 copy-start.2
  270.1 4.9 %copy-start.1 = (pred[128,12808]{0,1:T(8,128)(4,1)S(1)}, pred[128,12808]{0,1:T(8,128)(4,1)}, u32[]{:S(2)}) copy-start(pred[128,12808]{0,1:T(8,128)(4,1)} %get-tuple-element.432) | copy-start | bytes 4918276 | tf_op jit(solution)/shard_map/while
  275.0 1.9 copy-start.2
  279.3 4.9 %copy-start.1 = (pred[128,12808]{0,1:T(8,128)(4,1)S(1)}, pred[128,12808]{0,1:T(8,128)(4,1)}, u32[]{:S(2)}) copy-start(pred[128,12808]{0,1:T(8,128)(4,1)} %get-tuple-element.432) | copy-start | bytes 4918276 | tf_op jit(solution)/shard_map/while
  284.2 1.9 copy-start.2
Sparse Core Ops, SparseCore 0:
  62.7 42.9 all-gather.1
where the time goes:
time: 302 us; the launch traced here: 296 us
  matrix products  114 us (38%)
  other arithmetic  87.1 us (29%)
  local copies, waits for them, and re-layouts  40 us (13%)
  waiting for transfers between devices  17 us (6%)
  between operations  15.5 us (5%)
  blocking collectives  13.3 us (4%)
  starting transfers between devices  8.55 us (3%)
    dot_general x8, matrix products, partial_head(): lax.dot_general(query_rows, key_rows, (((1,), (1,)), ((), ())), preferred...  39.2 us
    dot_general x8, matrix products, update(): jnp.einsum('grn,dn->grd', exponent.astype(jnp.bfloat16), value_rows, pref...  26.2 us
    unnamed x4, other arithmetic  24.4 us
    dot_general x8, matrix products, update(): jnp.einsum('grd,dn->grn', self_queries, key_rows, preferred_element_type=...  21.9 us
    dot_general x8, matrix products, partial_head(): jnp.dot(exponent.astype(jnp.bfloat16), value_rows, preferred_element_type...  18.9 us
    all_to_all x1, waiting for transfers between devices, on_device(): lax.all_to_all(kv_tile, 'enc', split_axis=1, concat_axis=0, tiled=True)  16.9 us
    reduce_sum x8, other arithmetic, update(): running_sum = running_sum * decay_factor + jnp.sum(exponent, axis=-1)  16.8 us
    all_to_all x3, local copies, waits for them, and re-layouts, on_device(): lax.all_to_all(kv_tile, 'enc', split_axis=1, concat_axis=0, tiled=True)  15.7 us
  transfers between devices with their start and end apart: 3, of which 1 were waited for; matrix products, arithmetic and copies ran while one was open for 35% of the time, Pallas kernels for 0%

commit v1 on v0

v1 whole, which is shorter than its diff:
```python
import functools
import math

import jax
import jax.numpy as jnp
from jax import lax
from jax.experimental import pallas as pl
from jax.experimental.pallas import tpu as pltpu
from jax.sharding import PartitionSpec as P

HD = 128
GROUP = 8
TOK = 128
WIDTH = GROUP * HD
STAT = 128
PACK = WIDTH + STAT
NEG = -1e30
EXP2_SCALE = math.log2(math.e) / math.sqrt(HD)
VMEM = 50 * 1024 * 1024
BF16 = jnp.bfloat16
F32 = jnp.float32


def params():
    return pltpu.CompilerParams(vmem_limit_bytes=VMEM)


def project_kernel(tiles_ref, x_ref, w_ref, o_ref, *, rows, step):
    live = lax.axis_index("enc") < tiles_ref[lax.axis_index("seq")]
    i = pl.program_id(0)

    @pl.when(live)
    def _():
        y = jnp.dot(x_ref[...], w_ref[...], preferred_element_type=F32).astype(BF16)
        row = lax.broadcasted_iota(jnp.int32, y.shape, 0) + i * step
        y = jnp.where(row < rows, y, jnp.zeros_like(y))
        for g in range(4):
            o_ref[g] = y[:, g * 2 * HD : (g + 1) * 2 * HD]


def project(tiles, x, w, padded, step):
    rows, depth = x.shape
    return pl.pallas_call(
        functools.partial(project_kernel, rows=rows, step=step),
        grid_spec=pltpu.PrefetchScalarGridSpec(
            num_scalar_prefetch=1,
            grid=(padded // step,),
            in_specs=[
                pl.BlockSpec((step, depth), lambda i, t: (i, 0)),
                pl.BlockSpec(w.shape, lambda i, t: (0, 0)),
            ],
            out_specs=pl.BlockSpec((4, step, 2 * HD), lambda i, t: (0, i, 0)),
        ),
        out_shape=jax.ShapeDtypeStruct((4, padded, 2 * HD), BF16),
        compiler_params=params(),
        cost_estimate=pl.CostEstimate(
            flops=2 * rows * depth * w.shape[1], bytes_accessed=10_000_000, transcendentals=0
        ),
        name="project",
    )(tiles, x, w)


def split_stat(lse):
    hi = lse.astype(BF16)
    rest = lse - hi.astype(F32)
    mid = rest.astype(BF16)
    low = (rest - mid.astype(F32)).astype(BF16)
    return hi, mid, low


def cross_kernel(tiles_ref, *refs, offsets, picks, rows, last_seq):
    count = len(offsets)
    q_refs = refs[:count]
    kv_hbm, o_ref, queries, kv, sems = refs[count:]
    enc = lax.axis_index("enc")
    seq = lax.axis_index("seq")
    live = enc < tiles_ref[seq]
    if last_seq is not None:
        live = live & (seq < last_seq)
    padded = kv.shape[1]

    @pl.when(jnp.logical_not(live))
    def _():
        o_ref[:, :, :WIDTH] = jnp.zeros((count, TOK, WIDTH), BF16)
        o_ref[:, :, WIDTH:] = jnp.full((count, TOK, STAT), NEG, BF16)

    @pl.when(live)
    def _():
        copies = []
        for b, offset in enumerate(offsets):
            copy = pltpu.make_async_copy(
                kv_hbm.at[lax.rem(enc + offset, 4)], kv.at[b], sems.at[b]
            )
            copy.start()
            copies.append(copy)
        for b in range(count):
            for h in range(GROUP):
                queries[b, h * TOK : (h + 1) * TOK] = q_refs[b][picks[b], :, h * HD : (h + 1) * HD]
        lanes = lax.broadcasted_iota(jnp.int32, (1, HD), 1)
        edge = jnp.where(lanes < rows - (padded - HD), 0.0, NEG)

        def one_block(b, carry):
            pltpu.make_async_copy(kv_hbm.at[0], kv.at[b], sems.at[b]).wait()
            keys = kv[b, :, :HD]
            values = jnp.concatenate([kv[b, :, HD:], jnp.ones((padded, HD), BF16)], 1)
            maxes = jnp.zeros((TOK, STAT), F32)
            sums = jnp.ones((TOK, STAT), F32)
            part = 4
            for c in range(GROUP // part):
                q = queries[b, c * part * TOK : (c + 1) * part * TOK]
                s = lax.dot_general(q, keys, (((1,), (1,)), ((), ())), preferred_element_type=F32)
                s = jnp.concatenate([s[:, : padded - HD], s[:, padded - HD :] + edge], 1)
                m = jnp.max(s, 1, keepdims=True)
                p = jnp.exp2((s - m) * EXP2_SCALE).astype(BF16)
                mixed = jnp.dot(p, values, preferred_element_type=F32)
                total = mixed[:, HD:]
                out = (mixed[:, :HD] * (1.0 / total)).astype(BF16)
                for a in range(part):
                    h = c * part + a
                    at = slice(a * TOK, (a + 1) * TOK)
                    o_ref[b, :, h * HD : (h + 1) * HD] = out[at]
                    here = lax.rem(lanes, GROUP) == h
                    maxes = jnp.where(here, m[at], maxes)
                    sums = jnp.where(here, total[at], sums)
            hi, mid, low = split_stat(maxes * EXP2_SCALE + jnp.log2(sums))
            stat = jnp.where(lanes < GROUP, hi, jnp.where(lanes < 2 * GROUP, mid, low))
            o_ref[b, :, WIDTH:] = stat
            return carry

        lax.fori_loop(0, count, one_block, 0)


def cross(tiles, sources, kv, offsets, rows, padded, last_seq=None):
    count = len(offsets)
    pairs = count * WIDTH * padded
    return pl.pallas_call(
        functools.partial(
            cross_kernel,
            offsets=offsets,
            picks=[0] * count,
            rows=rows,
            last_seq=last_seq,
        ),
        grid_spec=pltpu.PrefetchScalarGridSpec(
            num_scalar_prefetch=1,
            grid=(1,),
            in_specs=[
                pl.BlockSpec((1, TOK, WIDTH), functools.partial(lambda pick, i, t: (pick, 0, 0), pick))
                for _, pick in sources
            ]
            + [pl.BlockSpec(memory_space=pl.ANY)],
            out_specs=pl.BlockSpec((count, TOK, PACK), lambda i, t: (0, 0, 0)),
            scratch_shapes=[
                pltpu.VMEM((count, GROUP * TOK, HD), BF16),
                pltpu.VMEM((count, padded, 2 * HD), BF16),
                pltpu.SemaphoreType.DMA((count,)),
            ],
        ),
        out_shape=jax.ShapeDtypeStruct((count, TOK, PACK), BF16),
        compiler_params=params(),
        cost_estimate=pl.CostEstimate(
            flops=8 * pairs * HD, bytes_accessed=count * 1_400_000, transcendentals=pairs
        ),
        name="cross",
    )(tiles, *[a for a, _ in sources], kv)


def stat_of(packed):
    s = packed[:, WIDTH:].astype(F32)
    return s[:, :GROUP] + s[:, GROUP : 2 * GROUP] + s[:, 2 * GROUP : 3 * GROUP]


def merge_kernel(range_ref, own_ref, rest_ref, prev_ref, *o_refs):
    seq = lax.axis_index("seq")
    first = lax.broadcasted_iota(jnp.int32, (TOK, GROUP), 0) < TOK // 2
    sees = []
    for image in (seq, seq - 1):
        spans = [
            ((range_ref[c, 0] <= image) & (image < range_ref[c, 1])).astype(jnp.int32)
            for c in range(2)
        ]
        sees.append(jnp.where(first, spans[0], spans[1]) != 0)
    lanes = lax.broadcasted_iota(jnp.int32, (1, STAT), 1)
    for b in range(4):
        now = own_ref.at[0] if b == 0 else rest_ref.at[b - 1]
        before = prev_ref.at[b]
        l0 = jnp.where(sees[0], stat_of(now[...]), NEG)
        l1 = jnp.where(sees[1], stat_of(before[...]), NEG)
        top = jnp.maximum(l0, l1)
        w0 = jnp.exp2(l0 - top)
        w1 = jnp.exp2(l1 - top)
        total = w0 + w1
        w0 = w0 / total
        w1 = w1 / total
        lse = top + jnp.log2(total)
        stat = jnp.zeros((TOK, STAT), F32)
        for h in range(GROUP):
            at = slice(h * HD, (h + 1) * HD)
            o_refs[b][:, at] = (
                now[:, at].astype(F32) * w0[:, h : h + 1]
                + before[:, at].astype(F32) * w1[:, h : h + 1]
            ).astype(BF16)
            stat = jnp.where(lax.rem(lanes, GROUP) == h, lse[:, h : h + 1], stat)
        hi, mid, low = split_stat(stat)
        o_refs[b][:, WIDTH:] = jnp.where(
            lanes < GROUP, hi, jnp.where(lanes < 2 * GROUP, mid, low)
        )


def merge(image_range, own, rest, prev):
    whole = lambda shape: pl.BlockSpec(shape, lambda i, t: (0,) * len(shape))
    return pl.pallas_call(
        merge_kernel,
        grid_spec=pltpu.PrefetchScalarGridSpec(
            num_scalar_prefetch=1,
            grid=(1,),
            in_specs=[whole(own.shape), whole(rest.shape), whole(prev.shape)],
            out_specs=[whole((TOK, PACK))] * 4,
        ),
        out_shape=[jax.ShapeDtypeStruct((TOK, PACK), BF16)] * 4,
        compiler_params=params(),
        cost_estimate=pl.CostEstimate(flops=10_000_000, bytes_accessed=4_000_000, transcendentals=0),
        name="merge",
    )(image_range, own, rest, prev)


def finish_kernel(*refs):
    parts, o_ref = refs[:4], refs[4]
    stats = [stat_of(part[...]) for part in parts]
    top = functools.reduce(jnp.maximum, stats)
    weights = [jnp.exp2(s - top) for s in stats]
    total = functools.reduce(jnp.add, weights)
    weights = [w / total for w in weights]
    for h in range(GROUP):
        at = slice(h * HD, (h + 1) * HD)
        o_ref[:, at] = functools.reduce(
            jnp.add,
            [part[:, at].astype(F32) * w[:, h : h + 1] for part, w in zip(parts, weights)],
        ).astype(BF16)


def finish(parts):
    return pl.pallas_call(
        finish_kernel,
        out_shape=jax.ShapeDtypeStruct((TOK, WIDTH), BF16),
        compiler_params=params(),
        cost_estimate=pl.CostEstimate(flops=10_000_000, bytes_accessed=1_500_000, transcendentals=0),
        name="finish",
    )(*parts)


KEY_STEP = 512


def self_kernel(q_ref, near_ref, far_ref, core_near_ref, core_far_ref, o_ref, cache_ref, kv, sems):
    seq = lax.axis_index("seq")
    z = seq // 8
    y = lax.rem(seq // 2, 4)
    core = lax.rem(seq, 2)
    low = z < 2
    low_z = jnp.where(low, z, 3 - z)

    def fetch(slot, when_low, otherwise, half):
        target = kv.at[slot, pl.ds(half * 64, 64)]
        sem = sems.at[slot, half]

        @pl.when(low)
        def _():
            pltpu.make_async_copy(when_low, target, sem).start()

        @pl.when(jnp.logical_not(low))
        def _():
            pltpu.make_async_copy(otherwise, target, sem).start()

    fetch(0, near_ref, far_ref, 0)
    fetch(0, core_near_ref, core_far_ref, 1)
    fetch(1, far_ref, near_ref, 0)
    fetch(1, core_far_ref, core_near_ref, 1)

    def order(z_bit):
        at = lax.broadcasted_iota(jnp.int32, (HD, HD), 1)
        feature = lax.broadcasted_iota(jnp.int32, (HD, HD), 0)
        y_step = (at // 8) % 4
        y_step = y_step ^ (y_step // 2)
        held = (
            ((z_bit ^ ((at // 32) % 2)) * 64)
            + ((y ^ y_step) * 16)
            + ((core ^ (at // 64)) * 8)
            + at % 8
        )
        return (held == feature).astype(BF16)

    key_order = order(low_z)
    value_order = order(1 - low_z)
    parts = 2
    heads = GROUP // parts
    queries = []
    for c in range(parts):
        q = jnp.concatenate(
            [q_ref[:, (c * heads + a) * HD : (c * heads + a + 1) * HD] for a in range(heads)], 0
        )
        queries.append(jnp.dot(q, key_order, preferred_element_type=F32).astype(BF16))
    for slot in range(2):
        for half in range(2):
            pltpu.make_async_copy(
                near_ref, kv.at[slot, pl.ds(half * 64, 64)], sems.at[slot, half]
            ).wait()
    mine = pl.ds(pl.multiple_of(seq * TOK, TOK), TOK)
    for slot, permutation in ((0, key_order), (1, value_order)):
        cache_ref[0, slot * HD : (slot + 1) * HD, :] = jnp.dot(
            permutation, kv[slot, :, mine], preferred_element_type=F32
        ).astype(BF16)
    rows = heads * TOK
    row = lax.rem(lax.broadcasted_iota(jnp.int32, (rows, KEY_STEP), 0), TOK) + seq * TOK
    column = lax.broadcasted_iota(jnp.int32, (rows, KEY_STEP), 1)

    def step(j, states, masked):
        at = pl.ds(pl.multiple_of(j * KEY_STEP, KEY_STEP), KEY_STEP)
        keys = kv[0, :, at]
        values = jnp.concatenate([kv[1, :, at], jnp.ones((HD, KEY_STEP), BF16)], 0)
        out = []
        for c in range(parts):
            m, acc = states[c]
            s = jnp.dot(queries[c], keys, preferred_element_type=F32)
            if masked:
                s = jnp.where(column + j * KEY_STEP <= row, s, NEG)
            new = jnp.maximum(m, jnp.max(s, 1, keepdims=True))
            p = jnp.exp2((s - new) * EXP2_SCALE).astype(BF16)
            acc = acc * jnp.exp2((m - new) * EXP2_SCALE) + lax.dot_general(
                p, values, (((1,), (1,)), ((), ())), preferred_element_type=F32
            )
            out.append((new, acc))
        return tuple(out)

    states = tuple(
        (jnp.full((rows, 1), NEG, F32), jnp.zeros((rows, 2 * HD), F32)) for _ in range(parts)
    )
    full = (seq * TOK) // KEY_STEP
    states = lax.fori_loop(0, full, lambda j, st: step(j, st, False), states)
    states = step(full, states, True)
    for c in range(parts):
        acc = states[c][1]
        out = (acc[:, :HD] * (1.0 / acc[:, HD:])).astype(BF16)
        out = lax.dot_general(
            out, value_order, (((1,), (1,)), ((), ())), preferred_element_type=F32
        ).astype(BF16)
        for a in range(heads):
            h = c * heads + a
            o_ref[:, h * HD : (h + 1) * HD] = out[a * TOK : (a + 1) * TOK]


def self_attend(q, near, far, core_near, core_far):
    tokens = near.shape[1]
    anywhere = pl.BlockSpec(memory_space=pl.ANY)
    return pl.pallas_call(
        self_kernel,
        grid=(1,),
        in_specs=[pl.BlockSpec((TOK, WIDTH), lambda i: (0, 0))] + [anywhere] * 4,
        out_specs=[
            pl.BlockSpec((TOK, WIDTH), lambda i: (0, 0)),
            pl.BlockSpec((1, 2 * HD, TOK), lambda i: (0, 0, 0)),
        ],
        out_shape=[
            jax.ShapeDtypeStruct((TOK, WIDTH), BF16),
            jax.ShapeDtypeStruct((1, 2 * HD, TOK), BF16),
        ],
        scratch_shapes=[
            pltpu.VMEM((2, HD, tokens), BF16),
            pltpu.SemaphoreType.DMA((2, 2)),
        ],
        compiler_params=params(),
        cost_estimate=pl.CostEstimate(
            flops=8 * WIDTH * tokens * HD, bytes_accessed=3_000_000, transcendentals=WIDTH * tokens
        ),
        name="self_attend",
    )(q, near, far, core_near, core_far)


def along_enc(x, by):
    size = lax.axis_size("enc")
    return lax.ppermute(x, "enc", [(i, (i + by) % size) for i in range(size)])


def along_seq(x, target):
    return lax.ppermute(x, "seq", [(i, target(i)) for i in range(lax.axis_size("seq"))])


def on_device(enc_tiles, kv_weight, q_cross, q_self, self_cache, image_range, image_tiles):
    size = lax.axis_size("seq")
    rows = enc_tiles.shape[2]
    q_next = lax.ppermute(q_cross, "seq", [(i + 1, i) for i in range(size - 1)])
    cache = self_cache[0]
    got = along_seq(cache, lambda i: i ^ 2)
    cache = jnp.concatenate([cache, got], 0)
    kv = project(image_tiles, enc_tiles[0, 0], kv_weight, 1664, 832)
    got = along_seq(cache, lambda i: i ^ 6)
    cache = jnp.concatenate([cache, got], 0)
    both = jnp.stack([q_cross, q_next])
    from_far = along_enc(both, 2)
    from_up = along_enc(both, 3)
    from_down = along_enc(both, 1)
    attend = functools.partial(cross, image_tiles, kv=kv, rows=rows, padded=1664)
    own = attend([(q_cross[None], 0)], offsets=(0,))
    got = along_seq(cache, lambda i: i ^ 8)
    near = jnp.concatenate([cache, got], 0)
    far = along_seq(near, lambda i: i ^ 24)
    core_near = along_seq(near, lambda i: i ^ 1)
    following = attend(
        [(q_next[None], 0), (from_up, 1), (from_down, 1), (from_far, 1)],
        offsets=(0, 1, 3, 2),
        last_seq=size - 1,
    )
    previous = lax.ppermute(following, "seq", [(i, i + 1) for i in range(size - 1)])
    core_far = along_seq(far, lambda i: i ^ 1)
    rest = attend([(from_up, 0), (from_down, 0), (from_far, 0)], offsets=(1, 3, 2))
    self_context, cache_seq = self_attend(q_self, near, far, core_near, core_far)
    mine, up, down, far_part = merge(image_range, own, rest, previous)
    parts = [mine, along_enc(far_part, 2), along_enc(up, 1), along_enc(down, 3)]
    return finish(parts), self_context, cache_seq


def solution(mesh):
    return jax.shard_map(
        on_device,
        mesh=mesh,
        in_specs=(
            P("seq", "enc", None, None),
            P(),
            P("seq", "enc"),
            P("seq", "enc"),
            P("enc", "seq", None),
            P("seq", None),
            P(),
        ),
        out_specs=(P("seq", "enc"), P("seq", "enc"), P("enc", None, "seq")),
        check_vma=False,
    )
```

time: 302 us -> 112 us (0.37); the launches traced: 296 us -> 112 us
  matrix products: 114 us -> 0 us
  other arithmetic: 87.1 us -> 1.91 us
  Pallas kernels: 0 us -> 44 us
  local copies, waits for them, and re-layouts: 40 us -> 2.42 us
  waiting for transfers between devices: 17 us -> 38.8 us
  starting transfers between devices: 8.55 us -> 23.8 us
  between operations: 15.5 us -> 0.8 us
  blocking collectives: 13.3 us -> 0 us
    dot_general x33 -> x0, matrix products: 114 us -> none  [the longest x8 39.2 us: partial_head(): lax.dot_general(query_rows, key_rows, (((1,), (1,)), ((), ())), preferred...]
    pallas_call x0 -> x7, Pallas kernels: none -> 44 us  [the longest x3 22.4 us: cross(): pl.pallas_call(functools.partial(cross_kernel, offsets=offsets, picks=[0]...]
    ppermute x1 -> x14, waiting for transfers between devices: 0.01 us -> 38.8 us  [the longest x6 21.4 us: along_seq(): lax.ppermute(x, 'seq', [(i, target(i)) for i in range(lax.axis_size('seq'...]
    reduce_sum x17 -> x0, other arithmetic: 31.9 us -> none  [the longest x8 16.8 us: update(): running_sum = running_sum * decay_factor + jnp.sum(exponent, axis=-1)]
    unnamed x4 -> x0, other arithmetic: 24.4 us -> none
    concatenate x2 -> x3, other arithmetic: 23.2 us -> 0.91 us  [the longest x2 0.87 us: on_device(): cache = jnp.concatenate([cache, got], 0)]
    all_to_all x5 -> x0, local copies, waits for them, and re-layouts: 20.8 us -> none  [the longest x3 15.7 us: on_device(): lax.all_to_all(kv_tile, 'enc', split_axis=1, concat_axis=0, tiled=True)]
    ppermute x1 -> x14, starting transfers between devices: 3.54 us -> 23.8 us  [the longest x6 10.4 us: along_seq(): lax.ppermute(x, 'seq', [(i, target(i)) for i in range(lax.axis_size('seq'...]
  transfers between devices with their start and end apart: 3 -> 14, of which waited for: 1 -> 5; matrix products, arithmetic and copies ran while one was open for 35% -> 2% of each run, Pallas kernels for 0% -> 38%
where the time goes in v1:
time: 112 us
  Pallas kernels  44 us (39%)
  waiting for transfers between devices  38.8 us (35%)
  starting transfers between devices  23.8 us (21%)
  local copies, waits for them, and re-layouts  2.42 us (2%)
  other arithmetic  1.91 us (2%)
    pallas_call x3, Pallas kernels, cross(): pl.pallas_call(functools.partial(cross_kernel, offsets=offsets, picks=[0]...  22.4 us
    ppermute x6, waiting for transfers between devices, along_seq(): lax.ppermute(x, 'seq', [(i, target(i)) for i in range(lax.axis_size('seq'...  21.4 us
    ppermute x6, waiting for transfers between devices, along_enc(): return lax.ppermute(x, 'enc', [(i, (i + by) % size) for i in range(size)])  15.1 us
    ppermute x6, starting transfers between devices, along_seq(): lax.ppermute(x, 'seq', [(i, target(i)) for i in range(lax.axis_size('seq'...  10.4 us
    pallas_call x1, Pallas kernels, self_attend(): pl.pallas_call(self_kernel, grid=(1,), in_specs=[pl.BlockSpec((TOK, WIDTH...  8.23 us
    pallas_call x1, Pallas kernels, project(): pl.pallas_call(functools.partial(project_kernel, rows=rows, step=step), g...  8.12 us
    ppermute x6, starting transfers between devices, along_enc(): return lax.ppermute(x, 'enc', [(i, (i + by) % size) for i in range(size)])  7.61 us
    pallas_call x1, Pallas kernels, merge(): pl.pallas_call(merge_kernel, grid_spec=pltpu.PrefetchScalarGridSpec(num_s...  3.79 us
  transfers between devices with their start and end apart: 14, of which 5 were waited for; matrix products, arithmetic and copies ran while one was open for 2% of the time, Pallas kernels for 38%

profile of v1, /device:TPU:65, one launch (start us, length us, event | category | flops | bytes accessed | tf_op | source)
XLA Modules:
  0.0 111.7 jit_solution(2725155614465881298)
XLA Ops:
  0.6 1.4 %collective-permute-start.8 = (bf16[8,4096]{1,0:T(8,128)(2,1)}, bf16[8,4096]{1,0:T(8,128)(2,1)S(1)}, u32[]{:S(2)}, u32[]{:S(2)}) collective-permute-start(bf16[8,4096]{1,0:T(8,128)(2,1)} %bitcast.8), channel_id=1, source_target_pairs={{0,8},{4,12},{8,0},{12,4},{16,24},{20,28},{24,16},{28,20},{32,40},... | collective-permute-start | bytes 196616 | tf_op jit(solution)/shard_map/ppermute | solution.py:385
  2.0 2.9 %collective-permute-start = (bf16[128,1024]{1,0:T(8,128)(2,1)}, bf16[128,1024]{1,0:T(8,128)(2,1)S(1)}, u32[]{:S(2)}, u32[]{:S(2)}) collective-permute-start(bf16[128,1024]{1,0:T(8,128)(2,1)} %param.9), channel_id=1, source_target_pairs={{4,0},{8,4},{12,8},{16,12},{20,16},{24,20},{28,24},{32,28},{36,32}... | collective-permute-start | bytes 786440 | tf_op jit(solution)/shard_map/ppermute | solution.py:391
  4.9 0.0 collective-permute-done.8
  4.9 0.9 pad_maximum_fusion.3
  5.7 2.0 %collective-permute-start.9 = (bf16[16,4096]{1,0:T(8,128)(2,1)S(1)}, bf16[16,4096]{1,0:T(8,128)(2,1)S(1)}, u32[]{:S(2)}, u32[]{:S(2)}) collective-permute-start(bf16[16,4096]{1,0:T(8,128)(2,1)S(1)} %pad_maximum_fusion.3), channel_id=1, source_target_pairs={{0,24},{4,28},{8,16},{12,20},{16,8},{20,12},{24,0},{28,4},{32,56},... | collective-permute-start | bytes 393224 | tf_op jit(solution)/shard_map/ppermute | solution.py:385
  7.7 2.2 %collective-permute-done = bf16[128,1024]{1,0:T(8,128)(2,1)S(1)} collective-permute-done((bf16[128,1024]{1,0:T(8,128)(2,1)}, bf16[128,1024]{1,0:T(8,128)(2,1)S(1)}, u32[]{:S(2)}, u32[]{:S(2)}) %collective-permute-start) | collective-permute-done | bytes 262176 | tf_op jit(solution)/shard_map/ppermute | solution.py:391
  9.9 1.0 pad_maximum_fusion
  10.9 2.5 %collective-permute-start.1 = (bf16[2,128,1024]{2,1,0:T(8,128)(2,1)S(1)}, bf16[2,128,1024]{2,1,0:T(8,128)(2,1)S(1)}, u32[]{:S(2)}, u32[]{:S(2)}) collective-permute-start(bf16[2,128,1024]{2,1,0:T(8,128)(2,1)S(1)} %pad_maximum_fusion), channel_id=1, source_target_pairs={{0,3},{1,0},{2,1},{3,2},{4,7},{5,4},{6,5},{7,6},{8,11},{9,8},{10,9... | collective-permute-start | bytes 1572872 | tf_op jit(solution)/shard_map/ppermute | solution.py:381
  13.5 1.7 %collective-permute-start.3 = (bf16[2,128,1024]{2,1,0:T(8,128)(2,1)S(1)}, bf16[2,128,1024]{2,1,0:T(8,128)(2,1)S(1)}, u32[]{:S(2)}, u32[]{:S(2)}) collective-permute-start(bf16[2,128,1024]{2,1,0:T(8,128)(2,1)S(1)} %pad_maximum_fusion), channel_id=1, source_target_pairs={{0,2},{1,3},{2,0},{3,1},{4,6},{5,7},{6,4},{7,5},{8,10},{9,11},{10,... | collective-permute-start | bytes 1572872 | tf_op jit(solution)/shard_map/ppermute | solution.py:381
  15.2 1.7 %copy-done.2 = bf16[1280,1024]{1,0:T(8,128)(2,1)S(1)} copy-done((bf16[1280,1024]{1,0:T(8,128)(2,1)S(1)}, bf16[1280,1024]{1,0:T(8,128)(2,1)}, u32[]{:S(2)}) %copy-start.2) | copy-done | bytes 2621464
  16.9 0.7 copy-done.4
  17.6 8.1 %project.1.refs_1_.refs_3_.refs_4_ = bf16[4,1664,256]{2,1,0:T(8,128)(2,1)} custom-call(s32[32]{0:T(128)S(1)} %copy-done.4, bf16[1601,1280]{1,0:T(8,128)(2,1)} %bitcast.12, bf16[1280,1024]{1,0:T(8,128)(2,1)S(1)} %copy-done.2), custom_call_target="tpu_custom_call" | custom-call | flops 4196925440 | bytes 10000000 | tf_op jit(solution)/shard_map/project/pallas_call | solution.py:43
  25.7 0.0 copy-start
  25.7 1.4 %collective-permute-start.10 = (bf16[32,4096]{1,0:T(8,128)(2,1)S(1)}, bf16[32,4096]{1,0:T(8,128)(2,1)S(1)}, u32[]{:S(2)}, u32[]{:S(2)}) collective-permute-start(bf16[32,4096]{1,0:T(8,128)(2,1)S(1)} %pad_maximum_fusion.2), channel_id=1, source_target_pairs={{0,32},{4,36},{8,40},{12,44},{16,48},{20,52},{24,56},{28,60},{32,0... | collective-permute-start | bytes 786440 | tf_op jit(solution)/shard_map/ppermute | solution.py:385
  27.2 0.4 collective-permute-done.2.refs_1_.refs_2_
  27.6 9.4 %collective-permute-done.3.refs_2_.refs_3_ = bf16[2,128,1024]{2,1,0:T(8,128)(2,1)S(1)} collective-permute-done((bf16[2,128,1024]{2,1,0:T(8,128)(2,1)S(1)}, bf16[2,128,1024]{2,1,0:T(8,128)(2,1)S(1)}, u32[]{:S(2)}, u32[]{:S(2)}) %collective-permute-start.3) | collective-permute-done | bytes 524320 | tf_op jit(solution)/shard_map/ppermute | solution.py:381
  36.9 10.7 %cross.5 = bf16[4,128,1152]{2,1,0:T(8,128)(2,1)S(1)} custom-call(s32[32]{0:T(128)S(1)} %copy-done.4, bf16[1,128,1024]{2,1,0:T(8,128)(2,1)S(1)} %bitcast.7, bf16[2,128,1024]{2,1,0:T(8,128)(2,1)S(1)} %collective-permute-done.1.refs_0_.refs_1_, bf16[2,128,1024]{2,1,0:T(8,128)(2,1)S(1)} %collective-permute-done.2.refs_1_.refs_2_, ...), custom_call_target="tpu_custom_call" | custom-call | flops 6979321856 | bytes 5600000 | tf_op jit(solution)/shard_map/cross/pallas_call | solution.py:136
  47.7 3.0 %collective-permute-start.4 = (bf16[4,128,1152]{2,1,0:T(8,128)(2,1)S(1)}, bf16[4,128,1152]{2,1,0:T(8,128)(2,1)S(1)}, u32[]{:S(2)}, u32[]{:S(2)}) collective-permute-start(bf16[4,128,1152]{2,1,0:T(8,128)(2,1)S(1)} %cross.5), channel_id=1, source_target_pairs={{0,4},{4,8},{8,12},{12,16},{16,20},{20,24},{24,28},{28,32},{32,36}... | collective-permute-start | bytes 3538952 | tf_op jit(solution)/shard_map/ppermute | solution.py:413
  50.7 0.1 collective-permute-start.11
  50.8 2.3 %collective-permute-start.12 = (bf16[64,4096]{1,0:T(8,128)(2,1)S(1)}, bf16[64,4096]{1,0:T(8,128)(2,1)S(1)}, u32[]{:S(2)}, u32[]{:S(2)}) collective-permute-start(bf16[64,4096]{1,0:T(8,128)(2,1)S(1)} %pad_maximum_fusion.1.near_ref), channel_id=1, source_target_pairs={{0,4},{4,0},{8,12},{12,8},{16,20},{20,16},{24,28},{28,24},{32,36},... | collective-permute-start | bytes 1572872 | tf_op jit(solution)/shard_map/ppermute | solution.py:385
  53.1 21.4 %collective-permute-done.11.far_ref = bf16[64,4096]{1,0:T(8,128)(2,1)S(1)} collective-permute-done((bf16[64,4096]{1,0:T(8,128)(2,1)S(1)}, bf16[64,4096]{1,0:T(8,128)(2,1)S(1)}, u32[]{:S(2)}, u32[]{:S(2)}) %collective-permute-start.11) | collective-permute-done | bytes 524320 | tf_op jit(solution)/shard_map/ppermute | solution.py:385
  74.6 3.2 %collective-permute-start.13 = (bf16[64,4096]{1,0:T(8,128)(2,1)S(1)}, bf16[64,4096]{1,0:T(8,128)(2,1)S(1)}, u32[]{:S(2)}, u32[]{:S(2)}) collective-permute-start(bf16[64,4096]{1,0:T(8,128)(2,1)S(1)} %collective-permute-done.11.far_ref), channel_id=1, source_target_pairs={{0,4},{4,0},{8,12},{12,8},{16,20},{20,16},{24,28},{28,24},{32,36},... | collective-permute-start | bytes 1572872 | tf_op jit(solution)/shard_map/ppermute | solution.py:385
  77.8 3.0 %cross.3.own_ref = bf16[1,128,1152]{2,1,0:T(8,128)(2,1)S(1)} custom-call(s32[32]{0:T(128)S(1)} %copy-done.4, bf16[1,128,1024]{2,1,0:T(8,128)(2,1)S(1)} %bitcast.5, bf16[4,1664,256]{2,1,0:T(8,128)(2,1)S(1)} %copy-done.5), custom_call_target="tpu_custom_call" | custom-call | flops 1744830464 | bytes 1400000 | tf_op jit(solution)/shard_map/cross/pallas_call | solution.py:136
  80.8 0.0 copy-start.1
  80.8 0.0 copy-start.3
  80.8 8.6 %cross.4.rest_ref = bf16[3,128,1152]{2,1,0:T(8,128)(2,1)S(1)} custom-call(s32[32]{0:T(128)S(1)} %copy-done.4, bf16[2,128,1024]{2,1,0:T(8,128)(2,1)S(1)} %collective-permute-done.1.refs_0_.refs_1_, bf16[2,128,1024]{2,1,0:T(8,128)(2,1)S(1)} %collective-permute-done.2.refs_1_.refs_2_, bf16[2,128,1024]{2,1,0:T(8,128)(2,1)S(1)} %collective-permute-done.3.refs_2_.refs_3_, ...), custom_call_target="tpu_custom_call" | custom-call | flops 5234491392 | bytes 4200000 | tf_op jit(solution)/shard_map/cross/pallas_call | solution.py:136
  89.5 3.8 %merge.1 = (bf16[128,1152]{1,0:T(8,128)(2,1)S(1)}, bf16[128,1152]{1,0:T(8,128)(2,1)S(1)}, bf16[128,1152]{1,0:T(8,128)(2,1)S(1)}, bf16[128,1152]{1,0:T(8,128)(2,1)S(1)}) custom-call(s32[2,2]{1,0:T(2,128)S(1)} %copy-done.1, bf16[1,128,1152]{2,1,0:T(8,128)(2,1)S(1)} %cross.3.own_ref, bf16[3,128,1152]{2,1,0:T(8,128)(2,1)S(1)} %cross.4.rest_ref, ...), custom_call_target="tpu_custom_call" | custom-call | flops 10000000 | bytes 4000000 | tf_op jit(solution)/shard_map/merge/pallas_call | solution.py:212
  93.3 0.7 collective-permute-start.5
  93.9 2.7 %collective-permute-start.7 = (bf16[128,1152]{1,0:T(8,128)(2,1)S(1)}, bf16[128,1152]{1,0:T(8,128)(2,1)S(1)}, u32[]{:S(2)}, u32[]{:S(2)}) collective-permute-start(bf16[128,1152]{1,0:T(8,128)(2,1)S(1)} %get-tuple-element.12), channel_id=1, source_target_pairs={{0,3},{1,0},{2,1},{3,2},{4,7},{5,4},{6,5},{7,6},{8,11},{9,8},{10,9... | collective-permute-start | bytes 884744 | tf_op jit(solution)/shard_map/ppermute | solution.py:381
  96.6 8.2 %self_attend.1 = (bf16[128,1024]{1,0:T(8,128)(2,1)}, bf16[1,256,128]{2,1,0:T(8,128)(2,1)}) custom-call(bf16[128,1024]{1,0:T(8,128)(2,1)S(1)} %copy-done.3, bf16[64,4096]{1,0:T(8,128)(2,1)S(1)} %pad_maximum_fusion.1.near_ref, bf16[64,4096]{1,0:T(8,128)(2,1)S(1)} %collective-permute-done.11.far_ref, ...), custom_call_target="tpu_custom_call" | custom-call | flops 4294967296 | bytes 3000000 | tf_op jit(solution)/shard_map/self_attend/pallas_call | solution.py:355
  104.8 5.3 %collective-permute-done.6.refs_2_ = bf16[128,1152]{1,0:T(8,128)(2,1)S(1)} collective-permute-done((bf16[128,1152]{1,0:T(8,128)(2,1)S(1)}, bf16[128,1152]{1,0:T(8,128)(2,1)S(1)}, u32[]{:S(2)}, u32[]{:S(2)}) %collective-permute-start.6) | collective-permute-done | bytes 294944 | tf_op jit(solution)/shard_map/ppermute | solution.py:381
  110.2 1.5 %finish.1 = bf16[128,1024]{1,0:T(8,128)(2,1)} custom-call(bf16[128,1152]{1,0:T(8,128)(2,1)S(1)} %get-tuple-element.9.refs_0_, bf16[128,1152]{1,0:T(8,128)(2,1)S(1)} %collective-permute-done.5.refs_1_, bf16[128,1152]{1,0:T(8,128)(2,1)S(1)} %collective-permute-done.6.refs_2_, bf16[128,1152]{1,0:T(8,128)(2,1)S(1)} %collective-permute-done.7.refs_3_), custom_call_target="tpu_custom_call" | custom-call | flops 10000000 | bytes 1500000 | tf_op jit(solution)/shard_map/finish/pallas_call | solution.py:243
  (21 shorter events, 0.1 us)
Async XLA Ops:
  0.6 4.2 %collective-permute-start.8 = (bf16[8,4096]{1,0:T(8,128)(2,1)}, bf16[8,4096]{1,0:T(8,128)(2,1)S(1)}, u32[]{:S(2)}, u32[]{:S(2)}) collective-permute-start(bf16[8,4096]{1,0:T(8,128)(2,1)} %bitcast.8), channel_id=1, source_target_pairs={{0,8},{4,12},{8,0},{12,4},{16,24},{20,28},{24,16},{28,20},{32,40},... | collective-permute-start | bytes 196616 | tf_op jit(solution)/shard_map/ppermute | solution.py:385
  2.0 7.9 %collective-permute-start = (bf16[128,1024]{1,0:T(8,128)(2,1)}, bf16[128,1024]{1,0:T(8,128)(2,1)S(1)}, u32[]{:S(2)}, u32[]{:S(2)}) collective-permute-start(bf16[128,1024]{1,0:T(8,128)(2,1)} %param.9), channel_id=1, source_target_pairs={{4,0},{8,4},{12,8},{16,12},{20,16},{24,20},{28,24},{32,28},{36,32}... | collective-permute-start | bytes 786440 | tf_op jit(solution)/shard_map/ppermute | solution.py:391
  5.7 20.0 %collective-permute-start.9 = (bf16[16,4096]{1,0:T(8,128)(2,1)S(1)}, bf16[16,4096]{1,0:T(8,128)(2,1)S(1)}, u32[]{:S(2)}, u32[]{:S(2)}) collective-permute-start(bf16[16,4096]{1,0:T(8,128)(2,1)S(1)} %pad_maximum_fusion.3), channel_id=1, source_target_pairs={{0,24},{4,28},{8,16},{12,20},{16,8},{20,12},{24,0},{28,4},{32,56},... | collective-permute-start | bytes 393224 | tf_op jit(solution)/shard_map/ppermute | solution.py:385
  10.9 16.3 %collective-permute-start.1 = (bf16[2,128,1024]{2,1,0:T(8,128)(2,1)S(1)}, bf16[2,128,1024]{2,1,0:T(8,128)(2,1)S(1)}, u32[]{:S(2)}, u32[]{:S(2)}) collective-permute-start(bf16[2,128,1024]{2,1,0:T(8,128)(2,1)S(1)} %pad_maximum_fusion), channel_id=1, source_target_pairs={{0,3},{1,0},{2,1},{3,2},{4,7},{5,4},{6,5},{7,6},{8,11},{9,8},{10,9... | collective-permute-start | bytes 1572872 | tf_op jit(solution)/shard_map/ppermute | solution.py:381
  13.4 14.1 %collective-permute-start.2 = (bf16[2,128,1024]{2,1,0:T(8,128)(2,1)S(1)}, bf16[2,128,1024]{2,1,0:T(8,128)(2,1)S(1)}, u32[]{:S(2)}, u32[]{:S(2)}) collective-permute-start(bf16[2,128,1024]{2,1,0:T(8,128)(2,1)S(1)} %pad_maximum_fusion), channel_id=1, source_target_pairs={{0,1},{1,2},{2,3},{3,0},{4,5},{5,6},{6,7},{7,4},{8,9},{9,10},{10,1... | collective-permute-start | bytes 1572872 | tf_op jit(solution)/shard_map/ppermute | solution.py:381
  13.5 23.5 %collective-permute-start.3 = (bf16[2,128,1024]{2,1,0:T(8,128)(2,1)S(1)}, bf16[2,128,1024]{2,1,0:T(8,128)(2,1)S(1)}, u32[]{:S(2)}, u32[]{:S(2)}) collective-permute-start(bf16[2,128,1024]{2,1,0:T(8,128)(2,1)S(1)} %pad_maximum_fusion), channel_id=1, source_target_pairs={{0,2},{1,3},{2,0},{3,1},{4,6},{5,7},{6,4},{7,5},{8,10},{9,11},{10,... | collective-permute-start | bytes 1572872 | tf_op jit(solution)/shard_map/ppermute | solution.py:381
  15.2 1.7 %copy-start.2 = (bf16[1280,1024]{1,0:T(8,128)(2,1)S(1)}, bf16[1280,1024]{1,0:T(8,128)(2,1)}, u32[]{:S(2)}) copy-start(bf16[1280,1024]{1,0:T(8,128)(2,1)} %w_ref.1) | copy-start | bytes 7864324
  16.9 0.7 copy-start.4
  17.6 8.1 %copy-start.6 = (bf16[1,8,4096]{2,1,0:T(8,128)(2,1)S(1)}, bf16[1,8,4096]{2,1,0:T(8,128)(2,1)}, u32[]{:S(2)}) copy-start(bf16[1,8,4096]{2,1,0:T(8,128)(2,1)} %param.11) | copy-start | bytes 196612
  25.7 52.0 %copy-start = (bf16[128,1024]{1,0:T(8,128)(2,1)S(1)}, bf16[128,1024]{1,0:T(8,128)(2,1)}, u32[]{:S(2)}) copy-start(bf16[128,1024]{1,0:T(8,128)(2,1)} %param.9) | copy-start | bytes 786436
  25.7 52.0 %copy-start.5 = (bf16[4,1664,256]{2,1,0:T(8,128)(2,1)S(1)}, bf16[4,1664,256]{2,1,0:T(8,128)(2,1)}, u32[]{:S(2)}) copy-start(bf16[4,1664,256]{2,1,0:T(8,128)(2,1)} %project.1.refs_1_.refs_3_.refs_4_) | copy-start | bytes 10223620
  25.7 24.9 %collective-permute-start.10 = (bf16[32,4096]{1,0:T(8,128)(2,1)S(1)}, bf16[32,4096]{1,0:T(8,128)(2,1)S(1)}, u32[]{:S(2)}, u32[]{:S(2)}) collective-permute-start(bf16[32,4096]{1,0:T(8,128)(2,1)S(1)} %pad_maximum_fusion.2), channel_id=1, source_target_pairs={{0,32},{4,36},{8,40},{12,44},{16,48},{20,52},{24,56},{28,60},{32,0... | collective-permute-start | bytes 786440 | tf_op jit(solution)/shard_map/ppermute | solution.py:385
  47.7 41.8 %collective-permute-start.4 = (bf16[4,128,1152]{2,1,0:T(8,128)(2,1)S(1)}, bf16[4,128,1152]{2,1,0:T(8,128)(2,1)S(1)}, u32[]{:S(2)}, u32[]{:S(2)}) collective-permute-start(bf16[4,128,1152]{2,1,0:T(8,128)(2,1)S(1)} %cross.5), channel_id=1, source_target_pairs={{0,4},{4,8},{8,12},{12,16},{16,20},{20,24},{24,28},{28,32},{32,36}... | collective-permute-start | bytes 3538952 | tf_op jit(solution)/shard_map/ppermute | solution.py:413
  50.7 23.9 %collective-permute-start.11 = (bf16[64,4096]{1,0:T(8,128)(2,1)S(1)}, bf16[64,4096]{1,0:T(8,128)(2,1)S(1)}, u32[]{:S(2)}, u32[]{:S(2)}) collective-permute-start(bf16[64,4096]{1,0:T(8,128)(2,1)S(1)} %pad_maximum_fusion.1.near_ref), channel_id=1, source_target_pairs={{0,96},{4,100},{8,104},{12,108},{16,112},{20,116},{24,120},{28,124... | collective-permute-start | bytes 1572872 | tf_op jit(solution)/shard_map/ppermute | solution.py:385
  50.8 45.8 %collective-permute-start.12 = (bf16[64,4096]{1,0:T(8,128)(2,1)S(1)}, bf16[64,4096]{1,0:T(8,128)(2,1)S(1)}, u32[]{:S(2)}, u32[]{:S(2)}) collective-permute-start(bf16[64,4096]{1,0:T(8,128)(2,1)S(1)} %pad_maximum_fusion.1.near_ref), channel_id=1, source_target_pairs={{0,4},{4,0},{8,12},{12,8},{16,20},{20,16},{24,28},{28,24},{32,36},... | collective-permute-start | bytes 1572872 | tf_op jit(solution)/shard_map/ppermute | solution.py:385
  74.6 22.0 %collective-permute-start.13 = (bf16[64,4096]{1,0:T(8,128)(2,1)S(1)}, bf16[64,4096]{1,0:T(8,128)(2,1)S(1)}, u32[]{:S(2)}, u32[]{:S(2)}) collective-permute-start(bf16[64,4096]{1,0:T(8,128)(2,1)S(1)} %collective-permute-done.11.far_ref), channel_id=1, source_target_pairs={{0,4},{4,0},{8,12},{12,8},{16,20},{20,16},{24,28},{28,24},{32,36},... | collective-permute-start | bytes 1572872 | tf_op jit(solution)/shard_map/ppermute | solution.py:385
  80.8 8.7 %copy-start.1 = (s32[2,2]{1,0:T(2,128)S(1)}, s32[2,2]{1,0:T(2,128)}, u32[]{:S(2)}) copy-start(s32[2,2]{1,0:T(2,128)} %range_ref.1) | copy-start | bytes 52
  80.8 15.8 %copy-start.3 = (bf16[128,1024]{1,0:T(8,128)(2,1)S(1)}, bf16[128,1024]{1,0:T(8,128)(2,1)}, u32[]{:S(2)}) copy-start(bf16[128,1024]{1,0:T(8,128)(2,1)} %q_ref.1) | copy-start | bytes 786436
  93.3 11.6 %collective-permute-start.5 = (bf16[128,1152]{1,0:T(8,128)(2,1)S(1)}, bf16[128,1152]{1,0:T(8,128)(2,1)S(1)}, u32[]{:S(2)}, u32[]{:S(2)}) collective-permute-start(bf16[128,1152]{1,0:T(8,128)(2,1)S(1)} %get-tuple-element.10), channel_id=1, source_target_pairs={{0,2},{1,3},{2,0},{3,1},{4,6},{5,7},{6,4},{7,5},{8,10},{9,11},{10,... | collective-permute-start | bytes 884744 | tf_op jit(solution)/shard_map/ppermute | solution.py:381
  93.9 16.3 %collective-permute-start.6 = (bf16[128,1152]{1,0:T(8,128)(2,1)S(1)}, bf16[128,1152]{1,0:T(8,128)(2,1)S(1)}, u32[]{:S(2)}, u32[]{:S(2)}) collective-permute-start(bf16[128,1152]{1,0:T(8,128)(2,1)S(1)} %get-tuple-element.11), channel_id=1, source_target_pairs={{0,1},{1,2},{2,3},{3,0},{4,5},{5,6},{6,7},{7,4},{8,9},{9,10},{10,1... | collective-permute-start | bytes 884744 | tf_op jit(solution)/shard_map/ppermute | solution.py:381
  93.9 16.3 %collective-permute-start.7 = (bf16[128,1152]{1,0:T(8,128)(2,1)S(1)}, bf16[128,1152]{1,0:T(8,128)(2,1)S(1)}, u32[]{:S(2)}, u32[]{:S(2)}) collective-permute-start(bf16[128,1152]{1,0:T(8,128)(2,1)S(1)} %get-tuple-element.12), channel_id=1, source_target_pairs={{0,3},{1,0},{2,1},{3,2},{4,7},{5,4},{6,5},{7,6},{8,11},{9,8},{10,9... | collective-permute-start | bytes 884744 | tf_op jit(solution)/shard_map/ppermute | solution.py:381

commit v2 on v1

v2 whole, which is shorter than its diff:
```python
import functools
import math

import jax
import jax.numpy as jnp
from jax import lax
from jax.experimental import pallas as pl
from jax.experimental.pallas import tpu as pltpu
from jax.sharding import PartitionSpec as P

HD = 128
GROUP = 8
TOK = 128
WIDTH = GROUP * HD
STAT = 128
PACK = WIDTH + STAT
NEG = -1e30
EXP2_SCALE = math.log2(math.e) / math.sqrt(HD)
VMEM = 28 * 1024 * 1024
BF16 = jnp.bfloat16
F32 = jnp.float32
COST_UNIT = 1_150_000_000


def cost(microseconds):
    return pl.CostEstimate(
        flops=int(microseconds * COST_UNIT), bytes_accessed=1000, transcendentals=0
    )


def params(limit=VMEM):
    return pltpu.CompilerParams(vmem_limit_bytes=limit)


def stage_kernel(x_hbm, w_hbm, _, x_ref, w_ref, sems):
    copies = [
        pltpu.make_async_copy(x_hbm, x_ref, sems.at[0]),
        pltpu.make_async_copy(w_hbm, w_ref, sems.at[1]),
    ]
    for copy in copies:
        copy.start()
    for copy in copies:
        copy.wait()


def stage(x, w, after):
    anywhere = pl.BlockSpec(memory_space=pl.ANY)
    in_vmem = pl.BlockSpec(memory_space=pltpu.VMEM)
    return pl.pallas_call(
        stage_kernel,
        in_specs=[anywhere] * 3,
        out_specs=[in_vmem] * 2,
        out_shape=[jax.ShapeDtypeStruct(x.shape, BF16), jax.ShapeDtypeStruct(w.shape, BF16)],
        scratch_shapes=[pltpu.SemaphoreType.DMA((2,))],
        compiler_params=params(),
        cost_estimate=cost(4),
        name="stage",
    )(x, w, after)


def project_kernel(tiles_ref, x_ref, w_ref, *refs, offsets, step):
    o_refs = refs[-len(offsets) :]
    enc = lax.axis_index("enc")
    live = enc < tiles_ref[lax.axis_index("seq")]
    rows = x_ref.shape[0]
    sent = o_refs[0].shape[1]

    @pl.when(live)
    def _():
        for o_ref, group in zip(o_refs, offsets):
            for b, offset in enumerate(group):
                g = lax.rem(enc + offset, 4)
                w = w_ref[:, pl.ds(pl.multiple_of(g * 2 * HD, 2 * HD), 2 * HD)]
                for start in range(0, rows, step):
                    end = min(start + step, rows)
                    y = jnp.dot(x_ref[start:end], w, preferred_element_type=F32)
                    if end == rows:
                        y = jnp.concatenate([y, jnp.zeros((sent - rows, 2 * HD), F32)], 0)
                        end = sent
                    o_ref[b, start:end] = y.astype(BF16)


def project(tiles, x, w, after, offsets, sent, step):
    in_vmem = pl.BlockSpec(memory_space=pltpu.VMEM)
    return pl.pallas_call(
        functools.partial(project_kernel, offsets=offsets, step=step),
        in_specs=[pl.BlockSpec(memory_space=pltpu.SMEM), in_vmem, in_vmem]
        + [pl.BlockSpec(memory_space=pl.ANY)] * len(after),
        out_specs=[in_vmem for _ in offsets],
        out_shape=[jax.ShapeDtypeStruct((len(o), sent, 2 * HD), BF16) for o in offsets],
        compiler_params=params(),
        cost_estimate=cost(5.5),
        name="project",
    )(tiles, x, w, *after)


def split_stat(lse):
    hi = lse.astype(BF16)
    rest = lse - hi.astype(F32)
    mid = rest.astype(BF16)
    low = (rest - mid.astype(F32)).astype(BF16)
    return hi, mid, low


def cross_kernel(tiles_ref, range_ref, *refs, waits, count, picks, priors, outputs, rows, last):
    refs = refs[waits:]
    q_refs = refs[:count]
    kv_ref = refs[count]
    prior_ref = refs[count + 1] if priors else None
    o_refs = refs[-3 - outputs : -3]
    queries, kv, sems = refs[-3:]
    sent = kv_ref.shape[1]
    padded = kv.shape[1]
    seq = lax.axis_index("seq")
    live = lax.axis_index("enc") < tiles_ref[seq]
    each = count // outputs
    lanes = lax.broadcasted_iota(jnp.int32, (1, HD), 1)

    def sees(image, shape):
        spans = [
            ((range_ref[c, 0] <= image) & (image < range_ref[c, 1])).astype(jnp.int32)
            for c in range(2)
        ]
        token = lax.rem(lax.broadcasted_iota(jnp.int32, shape, 0), TOK)
        return jnp.where(token < TOK // 2, spans[0], spans[1]) != 0

    if not priors:
        live = live & (seq < last)

    @pl.when(jnp.logical_not(live))
    def _():
        for b in range(count):
            o_ref = o_refs[b // each]
            if priors:
                o_ref[b % each, :, :WIDTH] = prior_ref[priors[b], :, :WIDTH]
                o_ref[b % each, :, WIDTH:] = jnp.where(
                    sees(seq - 1, (TOK, STAT)), prior_ref[priors[b], :, WIDTH:].astype(F32), NEG
                ).astype(BF16)
            else:
                o_ref[b % each, :, :WIDTH] = jnp.zeros((TOK, WIDTH), BF16)
                o_ref[b % each, :, WIDTH:] = jnp.full((TOK, STAT), NEG, BF16)

    @pl.when(live)
    def _():
        def fetch(b):
            return pltpu.make_async_copy(
                kv_ref.at[picks[b]], kv.at[b, pl.ds(0, sent)], sems.at[b]
            )

        for b in range(count):
            fetch(b).start()
        for b in range(count):
            kv[b, sent:] = jnp.zeros((padded - sent, 2 * HD), BF16)
            for h in range(GROUP):
                queries[b, h * TOK : (h + 1) * TOK] = q_refs[b][0, :, h * HD : (h + 1) * HD]
        edge = jnp.where(lanes < rows - (padded - HD), 0.0, NEG)
        part = 4
        if priors:
            seen = sees(seq, (part * TOK, 1))
            seen_before = sees(seq - 1, (TOK, GROUP))

        for b in range(count):
            fetch(b).wait()
            o_ref, at_out = o_refs[b // each], b % each
            keys = kv[b, :, :HD]
            values = jnp.concatenate([kv[b, :, HD:], jnp.ones((padded, HD), BF16)], 1)
            if priors:
                before = jnp.where(seen_before, stat_of(prior_ref[priors[b]]), NEG)
            tops = jnp.zeros((TOK, STAT), F32)
            sums = jnp.ones((TOK, STAT), F32)
            for c in range(GROUP // part):
                q = queries[b, c * part * TOK : (c + 1) * part * TOK]
                s = lax.dot_general(q, keys, (((1,), (1,)), ((), ())), preferred_element_type=F32)
                s = jnp.concatenate([s[:, : padded - HD], s[:, padded - HD :] + edge], 1)
                m = jnp.max(s, 1, keepdims=True) * EXP2_SCALE
                if priors:
                    prior = jnp.concatenate(
                        [before[:, c * part + a : c * part + a + 1] for a in range(part)], 0
                    )
                    m = jnp.where(seen, jnp.maximum(m, prior), prior)
                p = jnp.exp2(s * EXP2_SCALE - m).astype(BF16)
                mixed = jnp.dot(p, values, preferred_element_type=F32)
                total = mixed[:, HD:]
                mixed = mixed[:, :HD]
                if priors:
                    share = jnp.exp2(prior - m)
                    total = jnp.where(seen, total, 0.0) + share
                    out = jnp.concatenate(
                        [
                            prior_ref[priors[b], :, (c * part + a) * HD : (c * part + a + 1) * HD]
                            for a in range(part)
                        ],
                        0,
                    ).astype(F32)
                    mixed = jnp.where(seen, mixed, 0.0) + out * share
                out = (mixed * (1.0 / total)).astype(BF16)
                for a in range(part):
                    h = c * part + a
                    at = slice(a * TOK, (a + 1) * TOK)
                    o_ref[at_out, :, h * HD : (h + 1) * HD] = out[at]
                    here = lax.rem(lanes, GROUP) == h
                    tops = jnp.where(here, m[at], tops)
                    sums = jnp.where(here, total[at], sums)
            hi, mid, low = split_stat(tops + jnp.log2(sums))
            o_ref[at_out, :, WIDTH:] = jnp.where(
                lanes < GROUP, hi, jnp.where(lanes < 2 * GROUP, mid, low)
            )


def cross(tiles, image_range, queries, kv, picks, rows, prior=None, priors=(), outputs=1, after=()):
    count = len(queries)
    sent = kv.shape[1]
    padded = -(-rows // HD) * HD
    each = count // outputs
    whole = lambda shape: pl.BlockSpec(shape, lambda i, t, r: (0,) * len(shape))
    return pl.pallas_call(
        functools.partial(
            cross_kernel,
            waits=len(after),
            count=count,
            picks=picks,
            priors=priors,
            outputs=outputs,
            rows=rows,
            last=lax.axis_size("seq") - 1,
        ),
        grid_spec=pltpu.PrefetchScalarGridSpec(
            num_scalar_prefetch=2,
            grid=(1,),
            in_specs=[pl.BlockSpec(memory_space=pl.ANY)] * len(after)
            + [
                pl.BlockSpec((1, TOK, WIDTH), functools.partial(lambda k, i, t, r: (k, 0, 0), k))
                for _, k in queries
            ]
            + [pl.BlockSpec(memory_space=pl.ANY)]
            + ([whole(prior.shape)] if priors else []),
            out_specs=[whole((each, TOK, PACK))] * outputs,
            scratch_shapes=[
                pltpu.VMEM((count, GROUP * TOK, HD), BF16),
                pltpu.VMEM((count, padded, 2 * HD), BF16),
                pltpu.SemaphoreType.DMA((count,)),
            ],
        ),
        out_shape=[jax.ShapeDtypeStruct((each, TOK, PACK), BF16)] * outputs,
        compiler_params=params(),
        cost_estimate=cost(2.9 * count),
        name="cross",
    )(
        tiles,
        image_range,
        *after,
        *[q if q.ndim == 3 else q[None] for q, _ in queries],
        kv,
        *([prior] if priors else []),
    )


def stat_of(packed):
    s = packed[:, WIDTH:].astype(F32)
    return s[:, :GROUP] + s[:, GROUP : 2 * GROUP] + s[:, 2 * GROUP : 3 * GROUP]


def finish_kernel(*refs):
    parts, o_ref = refs[:4], refs[4]
    stats = [stat_of(part[0]) for part in parts]
    top = functools.reduce(jnp.maximum, stats)
    weights = [jnp.exp2(s - top) for s in stats]
    total = functools.reduce(jnp.add, weights)
    weights = [w / total for w in weights]
    for h in range(GROUP):
        at = slice(h * HD, (h + 1) * HD)
        o_ref[:, at] = functools.reduce(
            jnp.add,
            [part[0, :, at].astype(F32) * w[:, h : h + 1] for part, w in zip(parts, weights)],
        ).astype(BF16)


def finish(parts):
    return pl.pallas_call(
        finish_kernel,
        out_shape=jax.ShapeDtypeStruct((TOK, WIDTH), BF16),
        compiler_params=params(),
        cost_estimate=cost(1.5),
        name="finish",
    )(*parts)


KEY_STEP = 1024


def self_kernel(q_ref, near_ref, far_ref, core_near_ref, core_far_ref, _, o_ref, cache_ref, kv, sems):
    seq = lax.axis_index("seq")
    z = seq // 8
    y = lax.rem(seq // 2, 4)
    core = lax.rem(seq, 2)
    low = z < 2
    low_z = jnp.where(low, z, 3 - z)

    def fetch(slot, when_low, otherwise, half):
        target = kv.at[slot, pl.ds(half * 64, 64)]
        sem = sems.at[slot, half]

        @pl.when(low)
        def _():
            pltpu.make_async_copy(when_low, target, sem).start()

        @pl.when(jnp.logical_not(low))
        def _():
            pltpu.make_async_copy(otherwise, target, sem).start()

    fetch(0, near_ref, far_ref, 0)
    fetch(0, core_near_ref, core_far_ref, 1)
    fetch(1, far_ref, near_ref, 0)
    fetch(1, core_far_ref, core_near_ref, 1)

    def order(z_bit):
        at = lax.broadcasted_iota(jnp.int32, (HD, HD), 1)
        feature = lax.broadcasted_iota(jnp.int32, (HD, HD), 0)
        y_step = (at // 8) % 4
        y_step = y_step ^ (y_step // 2)
        held = (
            ((z_bit ^ ((at // 32) % 2)) * 64)
            + ((y ^ y_step) * 16)
            + ((core ^ (at // 64)) * 8)
            + at % 8
        )
        return (held == feature).astype(BF16)

    key_order = order(low_z)
    value_order = order(1 - low_z)
    parts = 2
    heads = GROUP // parts
    queries = []
    for c in range(parts):
        q = jnp.concatenate(
            [q_ref[:, (c * heads + a) * HD : (c * heads + a + 1) * HD] for a in range(heads)], 0
        )
        queries.append(jnp.dot(q, key_order, preferred_element_type=F32).astype(BF16))
    for slot in range(2):
        for half in range(2):
            pltpu.make_async_copy(
                near_ref, kv.at[slot, pl.ds(half * 64, 64)], sems.at[slot, half]
            ).wait()
    mine = pl.ds(pl.multiple_of(seq * TOK, TOK), TOK)
    for slot, permutation in ((0, key_order), (1, value_order)):
        cache_ref[0, slot * HD : (slot + 1) * HD, :] = jnp.dot(
            permutation, kv[slot, :, mine], preferred_element_type=F32
        ).astype(BF16)
    rows = heads * TOK
    row = lax.rem(lax.broadcasted_iota(jnp.int32, (rows, KEY_STEP), 0), TOK) + seq * TOK
    column = lax.broadcasted_iota(jnp.int32, (rows, KEY_STEP), 1)

    def step(j, states, masked):
        at = pl.ds(pl.multiple_of(j * KEY_STEP, KEY_STEP), KEY_STEP)
        keys = kv[0, :, at]
        values = jnp.concatenate([kv[1, :, at], jnp.ones((HD, KEY_STEP), BF16)], 0)
        out = []
        for c in range(parts):
            m, acc = states[c]
            s = jnp.dot(queries[c], keys, preferred_element_type=F32)
            if masked:
                s = jnp.where(column + j * KEY_STEP <= row, s, NEG)
            new = jnp.maximum(m, jnp.max(s, 1, keepdims=True))
            p = jnp.exp2((s - new) * EXP2_SCALE).astype(BF16)
            acc = acc * jnp.exp2((m - new) * EXP2_SCALE) + lax.dot_general(
                p, values, (((1,), (1,)), ((), ())), preferred_element_type=F32
            )
            out.append((new, acc))
        return tuple(out)

    states = tuple(
        (jnp.full((rows, 1), NEG, F32), jnp.zeros((rows, 2 * HD), F32)) for _ in range(parts)
    )
    full = (seq * TOK) // KEY_STEP
    states = lax.fori_loop(0, full, lambda j, st: step(j, st, False), states)
    states = step(full, states, True)
    for c in range(parts):
        acc = states[c][1]
        out = (acc[:, :HD] * (1.0 / acc[:, HD:])).astype(BF16)
        out = lax.dot_general(
            out, value_order, (((1,), (1,)), ((), ())), preferred_element_type=F32
        ).astype(BF16)
        for a in range(heads):
            h = c * heads + a
            o_ref[:, h * HD : (h + 1) * HD] = out[a * TOK : (a + 1) * TOK]


def self_attend(q, near, far, core_near, core_far, after):
    tokens = near.shape[1]
    anywhere = pl.BlockSpec(memory_space=pl.ANY)
    return pl.pallas_call(
        self_kernel,
        grid=(1,),
        in_specs=[pl.BlockSpec((TOK, WIDTH), lambda i: (0, 0))] + [anywhere] * 5,
        out_specs=[
            pl.BlockSpec((TOK, WIDTH), lambda i: (0, 0)),
            pl.BlockSpec((1, 2 * HD, TOK), lambda i: (0, 0, 0)),
        ],
        out_shape=[
            jax.ShapeDtypeStruct((TOK, WIDTH), BF16),
            jax.ShapeDtypeStruct((1, 2 * HD, TOK), BF16),
        ],
        scratch_shapes=[
            pltpu.VMEM((2, HD, tokens), BF16),
            pltpu.SemaphoreType.DMA((2, 2)),
        ],
        compiler_params=params(),
        cost_estimate=cost(6),
        name="self_attend",
    )(q, near, far, core_near, core_far, after)


def along_enc(x, by):
    size = lax.axis_size("enc")
    return lax.ppermute(x, "enc", [(i, (i + by) % size) for i in range(size)])


def along_seq(x, target):
    return lax.ppermute(x, "seq", [(i, target(i)) for i in range(lax.axis_size("seq"))])


def tied(x, *others):
    return lax.optimization_barrier((x, *others))[0]


def on_device(enc_tiles, kv_weight, q_cross, q_self, self_cache, image_range, image_tiles):
    rows = enc_tiles.shape[2]
    sent = -(-rows // 16) * 16
    size = lax.axis_size("seq")
    forward = lambda x: lax.ppermute(x, "seq", [(i, i + 1) for i in range(size - 1)])
    backward = lambda x: lax.ppermute(x, "seq", [(i + 1, i) for i in range(size - 1)])
    cache = self_cache[0]
    got = along_seq(cache, lambda i: i ^ 2)
    q_far = along_enc(q_cross, 2)
    q_up = along_enc(q_cross, 3)
    q_down = along_enc(q_cross, 1)
    q_next = backward(q_cross)
    cache = jnp.concatenate([cache, got], 0)
    tiles, weights = stage(enc_tiles[0, 0], kv_weight, cache)
    got = along_seq(cache, lambda i: i ^ 6)
    cache = jnp.concatenate([cache, tied(got, tiles)], 0)
    got = along_seq(cache, lambda i: i ^ 8)
    q_rest = jnp.stack([q_up, q_down, q_far])
    q_rest_next = backward(q_rest)
    (kv,) = project(
        image_tiles, tiles, weights, (cache, q_rest, q_next), ((0, 1, 3, 2),), sent, 416
    )
    near_cache = jnp.concatenate([cache, tied(got, kv)], 0)
    far_cache = along_seq(near_cache, lambda i: i ^ 24)
    core_near = along_seq(near_cache, lambda i: i ^ 1)
    attend = functools.partial(cross, image_tiles, image_range, kv=kv, rows=rows)
    (following,) = attend(
        [(q_next, 0), (q_rest_next, 0), (q_rest_next, 1), (q_rest_next, 2)],
        picks=(0, 1, 2, 3),
        after=(near_cache,),
    )
    prior = forward(following)
    core_far = along_seq(tied(far_cache, following), lambda i: i ^ 1)
    self_context, cache_seq = self_attend(
        q_self, near_cache, far_cache, core_near, core_far, following
    )
    (far,) = attend([(q_rest, 2)], picks=(3,), prior=prior, priors=(3,), after=(cache_seq,))
    far_got = along_enc(far, 2)
    up, down = attend(
        [(q_rest, 0), (q_rest, 1)],
        picks=(1, 2),
        prior=prior,
        priors=(1, 2),
        outputs=2,
        after=(far,),
    )
    up_got = along_enc(up, 1)
    down_got = along_enc(down, 3)
    (mine,) = attend([(q_cross, 0)], picks=(0,), prior=prior, priors=(0,), after=(up,))
    return finish([mine, far_got, up_got, down_got]), self_context, cache_seq


def solution(mesh):
    return jax.shard_map(
        on_device,
        mesh=mesh,
        in_specs=(
            P("seq", "enc", None, None),
            P(),
            P("seq", "enc"),
            P("seq", "enc"),
            P("enc", "seq", None),
            P("seq", None),
            P(),
        ),
        out_specs=(P("seq", "enc"), P("seq", "enc"), P("enc", None, "seq")),
        check_vma=False,
    )
```

time: 112 us -> 84.9 us (0.76)
  the two profiles are of different devices: /device:TPU:65 before, /device:TPU:102 now
where the time goes in v2:
time: 84.9 us; the launch traced here: 85.2 us
  Pallas kernels  42.1 us (50%)
  starting transfers between devices  21.8 us (26%)
  waiting for transfers between devices  14.7 us (17%)
  local copies, waits for them, and re-layouts  4.77 us (6%)
  other arithmetic  0.99 us (1%)
    pallas_call x4, Pallas kernels, cross(): pl.pallas_call(functools.partial(cross_kernel, waits=len(after), count=co...  24.4 us
    pallas_call x1, Pallas kernels, self_attend(): pl.pallas_call(self_kernel, grid=(1,), in_specs=[pl.BlockSpec((TOK, WIDTH...  10.4 us
    ppermute x6, starting transfers between devices, along_enc(): return lax.ppermute(x, 'enc', [(i, (i + by) % size) for i in range(size)])  9.11 us
    ppermute x2, starting transfers between devices, on_device(): lax.ppermute(x, 'seq', [(i + 1, i) for i in range(size - 1)])  6.11 us
    pallas_call x1, Pallas kernels, project(): pl.pallas_call(functools.partial(project_kernel, offsets=offsets, step=st...  5.02 us
    unnamed x16, local copies, waits for them, and re-layouts  4.77 us
    ppermute x6, starting transfers between devices, along_seq(): lax.ppermute(x, 'seq', [(i, target(i)) for i in range(lax.axis_size('seq'...  4.64 us
    ppermute x2, waiting for transfers between devices, on_device(): lax.ppermute(x, 'seq', [(i + 1, i) for i in range(size - 1)])  4.28 us
  transfers between devices with their start and end apart: 15, of which 8 were waited for; matrix products, arithmetic and copies ran while one was open for 1% of the time, Pallas kernels for 44%

profile of v2, /device:TPU:102, one launch (start us, length us, event | category | flops | bytes accessed | tf_op | source)
XLA Modules:
  0.0 85.2 jit_solution(6986179454008355101)
XLA Ops:
  0.6 1.7 %collective-permute-start = (bf16[8,4096]{1,0:T(8,128)(2,1)}, bf16[8,4096]{1,0:T(8,128)(2,1)S(1)}, u32[]{:S(2)}, u32[]{:S(2)}) collective-permute-start(bf16[8,4096]{1,0:T(8,128)(2,1)} %bitcast.10), channel_id=1, source_target_pairs={{0,8},{4,12},{8,0},{12,4},{16,24},{20,28},{24,16},{28,20},{32,40},... | collective-permute-start | bytes 196616 | tf_op jit(solution)/shard_map/ppermute | solution.py:419
  2.3 0.8 collective-permute-start.3
  3.1 2.4 %collective-permute-start.4 = (bf16[128,1024]{1,0:T(8,128)(2,1)}, bf16[128,1024]{1,0:T(8,128)(2,1)S(1)}, u32[]{:S(2)}, u32[]{:S(2)}) collective-permute-start(bf16[128,1024]{1,0:T(8,128)(2,1)} %param.9), channel_id=1, source_target_pairs={{0,1},{1,2},{2,3},{3,0},{4,5},{5,6},{6,7},{7,4},{8,9},{9,10},{10,1... | collective-permute-start | bytes 786440 | tf_op jit(solution)/shard_map/ppermute | solution.py:415
  5.5 0.2 collective-permute-start.5
  5.7 2.3 %collective-permute-start.6 = (bf16[128,1024]{1,0:T(8,128)(2,1)}, bf16[128,1024]{1,0:T(8,128)(2,1)S(1)}, u32[]{:S(2)}, u32[]{:S(2)}) collective-permute-start(bf16[128,1024]{1,0:T(8,128)(2,1)} %param.9), channel_id=1, source_target_pairs={{4,0},{8,4},{12,8},{16,12},{20,16},{24,20},{28,24},{32,28},{36,32}... | collective-permute-start | bytes 786440 | tf_op jit(solution)/shard_map/ppermute | solution.py:431
  8.1 0.9 pad_maximum_fusion.3._
  8.9 1.8 %collective-permute-start.1 = (bf16[16,4096]{1,0:T(8,128)(2,1)S(1)}, bf16[16,4096]{1,0:T(8,128)(2,1)S(1)}, u32[]{:S(2)}, u32[]{:S(2)}) collective-permute-start(bf16[16,4096]{1,0:T(8,128)(2,1)S(1)} %pad_maximum_fusion.3._), channel_id=1, source_target_pairs={{0,24},{4,28},{8,16},{12,20},{16,8},{20,12},{24,0},{28,4},{32,56},... | collective-permute-start | bytes 393224 | tf_op jit(solution)/shard_map/ppermute | solution.py:419
  10.8 2.2 %copy-done = bf16[1,1,1601,1280]{3,2,1,0:T(8,128)(2,1)S(1)} copy-done((bf16[1,1,1601,1280]{3,2,1,0:T(8,128)(2,1)S(1)}, bf16[1,1,1601,1280]{3,2,1,0:T(8,128)(2,1)}, u32[]{:S(2)}) %copy-start) | copy-done | bytes 4098584
  12.9 1.7 %copy-done.1 = bf16[1280,1024]{1,0:T(8,128)(2,1)S(1)} copy-done((bf16[1280,1024]{1,0:T(8,128)(2,1)S(1)}, bf16[1280,1024]{1,0:T(8,128)(2,1)}, u32[]{:S(2)}) %copy-start.1) | copy-done | bytes 2621464
  14.7 0.7 stage.1
  15.4 0.3 collective-permute-done.1
  15.7 0.5 collective-permute-start.2
  16.2 0.9 %collective-permute-done.3 = bf16[128,1024]{1,0:T(8,128)(2,1)S(1)} collective-permute-done((bf16[128,1024]{1,0:T(8,128)(2,1)}, bf16[128,1024]{1,0:T(8,128)(2,1)S(1)}, u32[]{:S(2)}, u32[]{:S(2)}) %collective-permute-start.3) | collective-permute-done | bytes 262176 | tf_op jit(solution)/shard_map/ppermute | solution.py:415
  17.2 3.8 %collective-permute-start.9 = (bf16[3,128,1024]{2,1,0:T(8,128)(2,1)S(1)}, bf16[3,128,1024]{2,1,0:T(8,128)(2,1)S(1)}, u32[]{:S(2)}, u32[]{:S(2)}) collective-permute-start(bf16[3,128,1024]{2,1,0:T(8,128)(2,1)S(1)} %pad_maximum_fusion.refs_1_.refs_2_), channel_id=1, source_target_pairs={{4,0},{8,4},{12,8},{16,12},{20,16},{24,20},{28,24},{32,28},{36,32}... | collective-permute-start | bytes 2359304 | tf_op jit(solution)/shard_map/ppermute | solution.py:431
  21.0 5.0 %project.1.refs_5_.refs_2_.refs_3_ = bf16[4,1616,256]{2,1,0:T(8,128)(2,1)S(1)} custom-call(s32[32]{0:T(128)S(1)} %copy-done.5, bf16[1601,1280]{1,0:T(8,128)(2,1)S(1)} %get-tuple-element.12.x_ref, bf16[1280,1024]{1,0:T(8,128)(2,1)S(1)} %get-tuple-element.14.w_ref, bf16[32,4096]{1,0:T(8,128)(2,1)S(1)} %pad_maximum_fusion.2.refs_0_, ...), custom_call_target="tpu_custom_call" | custom-call | flops 6325000192 | bytes 1000 | tf_op jit(solution)/shard_map/project/pallas_call | solution.py:85
  26.2 4.3 %collective-permute-done.9.refs_2_.refs_3_.refs_4_ = bf16[3,128,1024]{2,1,0:T(8,128)(2,1)S(1)} collective-permute-done((bf16[3,128,1024]{2,1,0:T(8,128)(2,1)S(1)}, bf16[3,128,1024]{2,1,0:T(8,128)(2,1)S(1)}, u32[]{:S(2)}, u32[]{:S(2)}) %collective-permute-start.9) | collective-permute-done | bytes 786464 | tf_op jit(solution)/shard_map/ppermute | solution.py:431
  30.5 10.9 %cross.4._ = bf16[4,128,1152]{2,1,0:T(8,128)(2,1)S(1)} custom-call(s32[32]{0:T(128)S(1)} %copy-done.5, s32[2,2]{1,0:T(2,128)S(1)} %copy-done.4, bf16[64,4096]{1,0:T(8,128)(2,1)S(1)} %pad_maximum_fusion.1.refs_0_.near_ref, bf16[1,128,1024]{2,1,0:T(8,128)(2,1)S(1)} %bitcast.9, bf16[3,128,1024]{2,1,0:T(8,128)(2,1)S(1)} %collective-permute-done.9.refs_2_.refs_3_.refs_4_, ...), custom_call_target="tpu_custom_call" | custom-call | flops 13340000256 | bytes 1000 | tf_op jit(solution)/shard_map/cross/pallas_call | solution.py:216
  41.4 1.9 %collective-permute-start.11 = (bf16[4,128,1152]{2,1,0:T(8,128)(2,1)S(1)}, bf16[4,128,1152]{2,1,0:T(8,128)(2,1)S(1)}, u32[]{:S(2)}, u32[]{:S(2)}) collective-permute-start(bf16[4,128,1152]{2,1,0:T(8,128)(2,1)S(1)} %cross.4._), channel_id=1, source_target_pairs={{0,4},{4,8},{8,12},{12,16},{16,20},{20,24},{24,28},{28,32},{32,36}... | collective-permute-start | bytes 3538952 | tf_op jit(solution)/shard_map/ppermute | solution.py:430
  43.4 0.5 collective-permute-start.10
  43.9 2.6 %collective-permute-done.8.core_near_ref = bf16[64,4096]{1,0:T(8,128)(2,1)S(1)} collective-permute-done((bf16[64,4096]{1,0:T(8,128)(2,1)S(1)}, bf16[64,4096]{1,0:T(8,128)(2,1)S(1)}, u32[]{:S(2)}, u32[]{:S(2)}) %collective-permute-start.8) | collective-permute-done | bytes 524320 | tf_op jit(solution)/shard_map/ppermute | solution.py:419
  46.5 0.7 collective-permute-done.10.core_far_ref
  47.3 10.4 %self_attend.1 = (bf16[128,1024]{1,0:T(8,128)(2,1)}, bf16[1,256,128]{2,1,0:T(8,128)(2,1)}) custom-call(bf16[128,1024]{1,0:T(8,128)(2,1)S(1)} %copy-done.2, bf16[64,4096]{1,0:T(8,128)(2,1)S(1)} %pad_maximum_fusion.1.refs_0_.near_ref, bf16[64,4096]{1,0:T(8,128)(2,1)S(1)} %collective-permute-done.7.far_ref, ...), custom_call_target="tpu_custom_call" | custom-call | flops 6899999744 | bytes 1000 | tf_op jit(solution)/shard_map/self_attend/pallas_call | solution.py:391
  57.7 3.3 %collective-permute-done.11.refs_3_.refs_4_ = bf16[4,128,1152]{2,1,0:T(8,128)(2,1)S(1)} collective-permute-done((bf16[4,128,1152]{2,1,0:T(8,128)(2,1)S(1)}, bf16[4,128,1152]{2,1,0:T(8,128)(2,1)S(1)}, u32[]{:S(2)}, u32[]{:S(2)}) %collective-permute-start.11) | collective-permute-done | bytes 1179680 | tf_op jit(solution)/shard_map/ppermute | solution.py:430
  61.0 0.8 copy-done.6
  61.9 3.5 %cross.5.refs_0_ = bf16[1,128,1152]{2,1,0:T(8,128)(2,1)S(1)} custom-call(s32[32]{0:T(128)S(1)} %copy-done.5, s32[2,2]{1,0:T(2,128)S(1)} %copy-done.4, bf16[1,256,128]{2,1,0:T(8,128)(2,1)S(1)} %copy-done.6, bf16[3,128,1024]{2,1,0:T(8,128)(2,1)S(1)} %pad_maximum_fusion.refs_1_.refs_2_, bf16[4,1616,256]{2,1,0:T(8,128)(2,1)S(1)} %project.1.refs_5_.refs_2_.refs_3_, ...), custom_call_target="tpu_custom_call" | custom-call | flops 3335000064 | bytes 1000 | tf_op jit(solution)/shard_map/cross/pallas_call | solution.py:216
  65.3 3.6 %collective-permute-start.12 = (bf16[1,128,1152]{2,1,0:T(8,128)(2,1)S(1)}, bf16[1,128,1152]{2,1,0:T(8,128)(2,1)S(1)}, u32[]{:S(2)}, u32[]{:S(2)}) collective-permute-start(bf16[1,128,1152]{2,1,0:T(8,128)(2,1)S(1)} %cross.5.refs_0_), channel_id=1, source_target_pairs={{0,2},{1,3},{2,0},{3,1},{4,6},{5,7},{6,4},{7,5},{8,10},{9,11},{10,... | collective-permute-start | bytes 884744 | tf_op jit(solution)/shard_map/ppermute | solution.py:415
  68.9 6.6 %cross.6 = (bf16[1,128,1152]{2,1,0:T(8,128)(2,1)S(1)}, bf16[1,128,1152]{2,1,0:T(8,128)(2,1)S(1)}) custom-call(s32[32]{0:T(128)S(1)} %copy-done.5, s32[2,2]{1,0:T(2,128)S(1)} %copy-done.4, bf16[1,128,1152]{2,1,0:T(8,128)(2,1)S(1)} %cross.5.refs_0_, bf16[3,128,1024]{2,1,0:T(8,128)(2,1)S(1)} %pad_maximum_fusion.refs_1_.refs_2_, ...), custom_call_target="tpu_custom_call" | custom-call | flops 6670000128 | bytes 1000 | tf_op jit(solution)/shard_map/cross/pallas_call | solution.py:216
  75.6 2.0 %collective-permute-start.14 = (bf16[1,128,1152]{2,1,0:T(8,128)(2,1)S(1)}, bf16[1,128,1152]{2,1,0:T(8,128)(2,1)S(1)}, u32[]{:S(2)}, u32[]{:S(2)}) collective-permute-start(bf16[1,128,1152]{2,1,0:T(8,128)(2,1)S(1)} %get-tuple-element.19), channel_id=1, source_target_pairs={{0,3},{1,0},{2,1},{3,2},{4,7},{5,4},{6,5},{7,6},{8,11},{9,8},{10,9... | collective-permute-start | bytes 884744 | tf_op jit(solution)/shard_map/ppermute | solution.py:415
  77.6 3.5 %cross.7.refs_0_ = bf16[1,128,1152]{2,1,0:T(8,128)(2,1)S(1)} custom-call(s32[32]{0:T(128)S(1)} %copy-done.5, s32[2,2]{1,0:T(2,128)S(1)} %copy-done.4, bf16[1,128,1152]{2,1,0:T(8,128)(2,1)S(1)} %get-tuple-element.18.refs_0_, bf16[1,128,1024]{2,1,0:T(8,128)(2,1)S(1)} %bitcast.8, bf16[4,1616,256]{2,1,0:T(8,128)(2,1)S(1)} %project.1.refs_5_.refs_2_.refs_3_, ...), custom_call_target="tpu_custom_call" | custom-call | flops 3335000064 | bytes 1000 | tf_op jit(solution)/shard_map/cross/pallas_call | solution.py:216
  81.1 1.2 %collective-permute-done.13.refs_2_ = bf16[1,128,1152]{2,1,0:T(8,128)(2,1)S(1)} collective-permute-done((bf16[1,128,1152]{2,1,0:T(8,128)(2,1)S(1)}, bf16[1,128,1152]{2,1,0:T(8,128)(2,1)S(1)}, u32[]{:S(2)}, u32[]{:S(2)}) %collective-permute-start.13) | collective-permute-done | bytes 294944 | tf_op jit(solution)/shard_map/ppermute | solution.py:415
  82.3 1.3 %collective-permute-done.14.refs_3_ = bf16[1,128,1152]{2,1,0:T(8,128)(2,1)S(1)} collective-permute-done((bf16[1,128,1152]{2,1,0:T(8,128)(2,1)S(1)}, bf16[1,128,1152]{2,1,0:T(8,128)(2,1)S(1)}, u32[]{:S(2)}, u32[]{:S(2)}) %collective-permute-start.14) | collective-permute-done | bytes 294944 | tf_op jit(solution)/shard_map/ppermute | solution.py:415
  83.6 1.5 %finish.1 = bf16[128,1024]{1,0:T(8,128)(2,1)} custom-call(bf16[1,128,1152]{2,1,0:T(8,128)(2,1)S(1)} %cross.7.refs_0_, bf16[1,128,1152]{2,1,0:T(8,128)(2,1)S(1)} %collective-permute-done.12.refs_1_, bf16[1,128,1152]{2,1,0:T(8,128)(2,1)S(1)} %collective-permute-done.13.refs_2_, bf16[1,128,1152]{2,1,0:T(8,128)(2,1)S(1)} %collective-permute-done.14.refs_3_), custom_call_target="tpu_custom_call" | custom-call | flops 1724999936 | bytes 1000 | tf_op jit(solution)/shard_map/finish/pallas_call | solution.py:279
  (26 shorter events, 0.4 us)
Async XLA Ops:
  0.6 7.4 %collective-permute-start = (bf16[8,4096]{1,0:T(8,128)(2,1)}, bf16[8,4096]{1,0:T(8,128)(2,1)S(1)}, u32[]{:S(2)}, u32[]{:S(2)}) collective-permute-start(bf16[8,4096]{1,0:T(8,128)(2,1)} %bitcast.10), channel_id=1, source_target_pairs={{0,8},{4,12},{8,0},{12,4},{16,24},{20,28},{24,16},{28,20},{32,40},... | collective-permute-start | bytes 196616 | tf_op jit(solution)/shard_map/ppermute | solution.py:419
  2.3 14.8 %collective-permute-start.3 = (bf16[128,1024]{1,0:T(8,128)(2,1)}, bf16[128,1024]{1,0:T(8,128)(2,1)S(1)}, u32[]{:S(2)}, u32[]{:S(2)}) collective-permute-start(bf16[128,1024]{1,0:T(8,128)(2,1)} %param.9), channel_id=1, source_target_pairs={{0,3},{1,0},{2,1},{3,2},{4,7},{5,4},{6,5},{7,6},{8,11},{9,8},{10,9... | collective-permute-start | bytes 786440 | tf_op jit(solution)/shard_map/ppermute | solution.py:415
  3.1 14.0 %collective-permute-start.4 = (bf16[128,1024]{1,0:T(8,128)(2,1)}, bf16[128,1024]{1,0:T(8,128)(2,1)S(1)}, u32[]{:S(2)}, u32[]{:S(2)}) collective-permute-start(bf16[128,1024]{1,0:T(8,128)(2,1)} %param.9), channel_id=1, source_target_pairs={{0,1},{1,2},{2,3},{3,0},{4,5},{5,6},{6,7},{7,4},{8,9},{9,10},{10,1... | collective-permute-start | bytes 786440 | tf_op jit(solution)/shard_map/ppermute | solution.py:415
  5.5 11.6 %collective-permute-start.5 = (bf16[128,1024]{1,0:T(8,128)(2,1)}, bf16[128,1024]{1,0:T(8,128)(2,1)S(1)}, u32[]{:S(2)}, u32[]{:S(2)}) collective-permute-start(bf16[128,1024]{1,0:T(8,128)(2,1)} %param.9), channel_id=1, source_target_pairs={{0,2},{1,3},{2,0},{3,1},{4,6},{5,7},{6,4},{7,5},{8,10},{9,11},{10,... | collective-permute-start | bytes 786440 | tf_op jit(solution)/shard_map/ppermute | solution.py:415
  5.7 15.3 %collective-permute-start.6 = (bf16[128,1024]{1,0:T(8,128)(2,1)}, bf16[128,1024]{1,0:T(8,128)(2,1)S(1)}, u32[]{:S(2)}, u32[]{:S(2)}) collective-permute-start(bf16[128,1024]{1,0:T(8,128)(2,1)} %param.9), channel_id=1, source_target_pairs={{4,0},{8,4},{12,8},{16,12},{20,16},{24,20},{28,24},{32,28},{36,32}... | collective-permute-start | bytes 786440 | tf_op jit(solution)/shard_map/ppermute | solution.py:431
  8.9 6.8 %collective-permute-start.1 = (bf16[16,4096]{1,0:T(8,128)(2,1)S(1)}, bf16[16,4096]{1,0:T(8,128)(2,1)S(1)}, u32[]{:S(2)}, u32[]{:S(2)}) collective-permute-start(bf16[16,4096]{1,0:T(8,128)(2,1)S(1)} %pad_maximum_fusion.3._), channel_id=1, source_target_pairs={{0,24},{4,28},{8,16},{12,20},{16,8},{20,12},{24,0},{28,4},{32,56},... | collective-permute-start | bytes 393224 | tf_op jit(solution)/shard_map/ppermute | solution.py:419
  10.8 2.2 %copy-start = (bf16[1,1,1601,1280]{3,2,1,0:T(8,128)(2,1)S(1)}, bf16[1,1,1601,1280]{3,2,1,0:T(8,128)(2,1)}, u32[]{:S(2)}) copy-start(bf16[1,1,1601,1280]{3,2,1,0:T(8,128)(2,1)} %param.7) | copy-start | bytes 12295684
  12.9 1.7 %copy-start.1 = (bf16[1280,1024]{1,0:T(8,128)(2,1)S(1)}, bf16[1280,1024]{1,0:T(8,128)(2,1)}, u32[]{:S(2)}) copy-start(bf16[1280,1024]{1,0:T(8,128)(2,1)} %w_hbm.1) | copy-start | bytes 7864324
  14.7 1.0 %copy-start.7 = (bf16[1,8,4096]{2,1,0:T(8,128)(2,1)S(1)}, bf16[1,8,4096]{2,1,0:T(8,128)(2,1)}, u32[]{:S(2)}) copy-start(bf16[1,8,4096]{2,1,0:T(8,128)(2,1)} %param.11) | copy-start | bytes 196612
  14.7 6.3 %copy-start.5 = (s32[32]{0:T(128)S(1)}, s32[32]{0:T(128)}, u32[]{:S(2)}) copy-start(s32[32]{0:T(128)} %tiles_ref.9) | copy-start | bytes 388
  15.7 10.3 %collective-permute-start.2 = (bf16[32,4096]{1,0:T(8,128)(2,1)S(1)}, bf16[32,4096]{1,0:T(8,128)(2,1)S(1)}, u32[]{:S(2)}, u32[]{:S(2)}) collective-permute-start(bf16[32,4096]{1,0:T(8,128)(2,1)S(1)} %pad_maximum_fusion.2.refs_0_), channel_id=1, source_target_pairs={{0,32},{4,36},{8,40},{12,44},{16,48},{20,52},{24,56},{28,60},{32,0... | collective-permute-start | bytes 786440 | tf_op jit(solution)/shard_map/ppermute | solution.py:419
  17.2 13.3 %collective-permute-start.9 = (bf16[3,128,1024]{2,1,0:T(8,128)(2,1)S(1)}, bf16[3,128,1024]{2,1,0:T(8,128)(2,1)S(1)}, u32[]{:S(2)}, u32[]{:S(2)}) collective-permute-start(bf16[3,128,1024]{2,1,0:T(8,128)(2,1)S(1)} %pad_maximum_fusion.refs_1_.refs_2_), channel_id=1, source_target_pairs={{4,0},{8,4},{12,8},{16,12},{20,16},{24,20},{28,24},{32,28},{36,32}... | collective-permute-start | bytes 2359304 | tf_op jit(solution)/shard_map/ppermute | solution.py:431
  21.0 9.5 %copy-start.4 = (s32[2,2]{1,0:T(2,128)S(1)}, s32[2,2]{1,0:T(2,128)}, u32[]{:S(2)}) copy-start(s32[2,2]{1,0:T(2,128)} %range_ref.7) | copy-start | bytes 52
  26.1 17.3 %collective-permute-start.7 = (bf16[64,4096]{1,0:T(8,128)(2,1)S(1)}, bf16[64,4096]{1,0:T(8,128)(2,1)S(1)}, u32[]{:S(2)}, u32[]{:S(2)}) collective-permute-start(bf16[64,4096]{1,0:T(8,128)(2,1)S(1)} %pad_maximum_fusion.1.refs_0_.near_ref), channel_id=1, source_target_pairs={{0,96},{4,100},{8,104},{12,108},{16,112},{20,116},{24,120},{28,124... | collective-permute-start | bytes 1572872 | tf_op jit(solution)/shard_map/ppermute | solution.py:419
  30.5 16.8 %copy-start.2 = (bf16[128,1024]{1,0:T(8,128)(2,1)S(1)}, bf16[128,1024]{1,0:T(8,128)(2,1)}, u32[]{:S(2)}) copy-start(bf16[128,1024]{1,0:T(8,128)(2,1)} %q_ref.1) | copy-start | bytes 786436
  41.4 19.6 %collective-permute-start.11 = (bf16[4,128,1152]{2,1,0:T(8,128)(2,1)S(1)}, bf16[4,128,1152]{2,1,0:T(8,128)(2,1)S(1)}, u32[]{:S(2)}, u32[]{:S(2)}) collective-permute-start(bf16[4,128,1152]{2,1,0:T(8,128)(2,1)S(1)} %cross.4._), channel_id=1, source_target_pairs={{0,4},{4,8},{8,12},{12,16},{16,20},{20,24},{24,28},{28,32},{32,36}... | collective-permute-start | bytes 3538952 | tf_op jit(solution)/shard_map/ppermute | solution.py:430
  43.3 3.2 %collective-permute-start.8 = (bf16[64,4096]{1,0:T(8,128)(2,1)S(1)}, bf16[64,4096]{1,0:T(8,128)(2,1)S(1)}, u32[]{:S(2)}, u32[]{:S(2)}) collective-permute-start(bf16[64,4096]{1,0:T(8,128)(2,1)S(1)} %pad_maximum_fusion.1.refs_0_.near_ref), channel_id=1, source_target_pairs={{0,4},{4,0},{8,12},{12,8},{16,20},{20,16},{24,28},{28,24},{32,36},... | collective-permute-start | bytes 1572872 | tf_op jit(solution)/shard_map/ppermute | solution.py:419
  43.4 3.8 %collective-permute-start.10 = (bf16[64,4096]{1,0:T(8,128)(2,1)S(1)}, bf16[64,4096]{1,0:T(8,128)(2,1)S(1)}, u32[]{:S(2)}, u32[]{:S(2)}) collective-permute-start(bf16[64,4096]{1,0:T(8,128)(2,1)S(1)} %collective-permute-done.7.far_ref), channel_id=1, source_target_pairs={{0,4},{4,0},{8,12},{12,8},{16,20},{20,16},{24,28},{28,24},{32,36},... | collective-permute-start | bytes 1572872 | tf_op jit(solution)/shard_map/ppermute | solution.py:419
  61.0 0.8 copy-start.6
  65.3 12.3 %copy-start.3 = (bf16[128,1024]{1,0:T(8,128)(2,1)S(1)}, bf16[128,1024]{1,0:T(8,128)(2,1)}, u32[]{:S(2)}) copy-start(bf16[128,1024]{1,0:T(8,128)(2,1)} %param.9) | copy-start | bytes 786436
  65.3 18.3 %collective-permute-start.12 = (bf16[1,128,1152]{2,1,0:T(8,128)(2,1)S(1)}, bf16[1,128,1152]{2,1,0:T(8,128)(2,1)S(1)}, u32[]{:S(2)}, u32[]{:S(2)}) collective-permute-start(bf16[1,128,1152]{2,1,0:T(8,128)(2,1)S(1)} %cross.5.refs_0_), channel_id=1, source_target_pairs={{0,2},{1,3},{2,0},{3,1},{4,6},{5,7},{6,4},{7,5},{8,10},{9,11},{10,... | collective-permute-start | bytes 884744 | tf_op jit(solution)/shard_map/ppermute | solution.py:415
  75.5 6.8 %collective-permute-start.13 = (bf16[1,128,1152]{2,1,0:T(8,128)(2,1)S(1)}, bf16[1,128,1152]{2,1,0:T(8,128)(2,1)S(1)}, u32[]{:S(2)}, u32[]{:S(2)}) collective-permute-start(bf16[1,128,1152]{2,1,0:T(8,128)(2,1)S(1)} %get-tuple-element.18.refs_0_), channel_id=1, source_target_pairs={{0,1},{1,2},{2,3},{3,0},{4,5},{5,6},{6,7},{7,4},{8,9},{9,10},{10,1... | collective-permute-start | bytes 884744 | tf_op jit(solution)/shard_map/ppermute | solution.py:415
  75.6 8.0 %collective-permute-start.14 = (bf16[1,128,1152]{2,1,0:T(8,128)(2,1)S(1)}, bf16[1,128,1152]{2,1,0:T(8,128)(2,1)S(1)}, u32[]{:S(2)}, u32[]{:S(2)}) collective-permute-start(bf16[1,128,1152]{2,1,0:T(8,128)(2,1)S(1)} %get-tuple-element.19), channel_id=1, source_target_pairs={{0,3},{1,0},{2,1},{3,2},{4,7},{5,4},{6,5},{7,6},{8,11},{9,8},{10,9... | collective-permute-start | bytes 884744 | tf_op jit(solution)/shard_map/ppermute | solution.py:415
